TPU v7x, 512 devices: a whole 4x4x16 slice. The times are simulated.
512 devices in a mesh: dp: 8 (over x, core), seq: 64 (over y, z).
Axes of the slice: x: 4, y: 4, z: 16, core: 2. Of those that a mesh axis runs over, the one named last changes fastest.
Arguments:
- query_raw: bfloat16 [8, 8192, 2560], P('dp', 'seq'), may hold values from -8 to 8
- key_raw: bfloat16 [8, 8192, 512], P('dp', 'seq'), may hold values from -8 to 8
- values: bfloat16 [8, 8192, 512], P('dp', 'seq'), may hold values from -6 to 6
- query_gain: float32 [128], replicated, may hold values from 0.5 to 5
- key_gain: float32 [128], replicated, may hold values from 0.5 to 5
- segment_ids: int32 [8, 8192], P('dp', 'seq'), may hold values from 0 to 15, never falling along the last dimension, each value on 1 to 896 neighbouring positions
- grad_attended: bfloat16 [8, 8192, 2560], P('dp', 'seq'), may hold values from -200 to 200
Outputs:
- attended: bfloat16 [8, 8192, 2560], P('dp', 'seq')
- grad_query_raw: bfloat16 [8, 8192, 2560], P('dp', 'seq')
- grad_key_raw: bfloat16 [8, 8192, 512], P('dp', 'seq')
- grad_values: bfloat16 [8, 8192, 512], P('dp', 'seq')
- grad_query_gain: float32 [128], replicated
- grad_key_gain: float32 [128], replicated
Inputs may be any that keep to these rules, and one draw needn't show every extreme that they name: `segment_ids`: within each pack ids start at 0 and never fall; every transcript holds 1 to 896 positions, and one holds exactly that many.
All inputs are finite; a program needn't handle non-finite values.
Results may differ from a plain program's by a relative error of at most 0.01.
The roundings to bfloat16 on the way count: a program that leaves them out, or rounds other values in their place, can miss the bound.
Values may be sent and summed in bfloat16 or wider, within the bound.
A program may use at most 64 MiB of HBM per device.

v0:
```python
import jax
import jax.numpy as jnp
from jax import lax
from jax.sharding import PartitionSpec as P

SPAN = 7


epsilon = 1e-06


def shifted(value, axis, steps):
    count = lax.axis_size(axis)
    initial, last = (max(0, -steps), min(count, count - steps))
    return lax.ppermute(value, axis, [(source, source + steps) for source in range(initial, last)])


def normalize(rows):
    inverse = lax.rsqrt(jnp.mean(rows * rows, axis=-1, keepdims=True) + epsilon)
    return (rows * inverse, inverse)


def norm_backward(grad, unit, inverse, gain):
    scaled = grad * gain
    return inverse * (scaled - unit * jnp.mean(scaled * unit, axis=-1, keepdims=True))


def visible_mask(seg_query, seg_window, tok_rows):
    query_pos = jnp.arange(tok_rows, dtype=jnp.int32)[:, None]
    key_pos = jnp.arange((SPAN + 1) * tok_rows, dtype=jnp.int32)[None, :] - SPAN * tok_rows
    return (seg_window[None, :] == seg_query[:, None]) & (key_pos <= query_pos)


def head_scores(queries, key_rows, visible):
    scaling = queries.shape[-1] ** (-0.5)
    scores = (
        jnp.einsum("tgh,wh->tgw", queries, key_rows, preferred_element_type=jnp.float32) * scaling
    )
    return jnp.where(visible[:, None, :], scores, -1e30)


def group_forward(queries, key_rows, value_rows, visible):
    scores = head_scores(queries, key_rows, visible)
    row_max = jnp.max(scores, axis=-1, keepdims=True)
    row_sum = jnp.sum(jnp.exp(scores - row_max), axis=-1, keepdims=True)
    log_sum = row_max + jnp.log(row_sum)
    weights = jnp.exp(scores - log_sum).astype(jnp.bfloat16)
    output = jnp.einsum("tgw,wh->tgh", weights, value_rows, preferred_element_type=jnp.float32)
    return (output, log_sum[..., 0])


def group_backward(queries, key_rows, value_rows, visible, log_sum, grad_out, correction):
    scaling = queries.shape[-1] ** (-0.5)
    scores = head_scores(queries, key_rows, visible)
    probs = jnp.exp(scores - log_sum[..., None])
    weights = probs.astype(jnp.bfloat16)
    grad_prob = jnp.einsum("tgh,wh->tgw", grad_out, value_rows, preferred_element_type=jnp.float32)
    grad_scores = (probs * (grad_prob - correction[..., None]) * scaling).astype(jnp.bfloat16)
    grad_query = jnp.einsum(
        "tgw,wh->tgh", grad_scores, key_rows, preferred_element_type=jnp.float32
    )
    grad_key = jnp.einsum("tgw,tgh->wh", grad_scores, queries, preferred_element_type=jnp.float32)
    grad_value = jnp.einsum("tgw,tgh->wh", weights, grad_out, preferred_element_type=jnp.float32)
    return (grad_query, grad_key, grad_value)


def device_block(query_norm, seg_query, key_window, value_window, seg_window, grad_out):
    tok_rows = query_norm.shape[0]
    visible = visible_mask(seg_query, seg_window, tok_rows)
    query_heads = jnp.moveaxis(query_norm, 1, 0)
    key_heads = jnp.moveaxis(key_window, 1, 0)
    value_heads = jnp.moveaxis(value_window, 1, 0)

    def forward_one(operands):
        return group_forward(operands[0], operands[1], operands[2], visible)

    output, log_sum = lax.map(forward_one, (query_heads, key_heads, value_heads))
    attended = jnp.moveaxis(output, 0, 1).astype(jnp.bfloat16)
    correction = jnp.sum(grad_out.astype(jnp.float32) * attended.astype(jnp.float32), axis=-1)
    grad_heads = jnp.moveaxis(grad_out, 1, 0)
    correction_heads = jnp.moveaxis(correction, 1, 0)

    def backward_one(operands):
        return group_backward(
            operands[0], operands[1], operands[2], visible, operands[3], operands[4], operands[5]
        )

    grad_query, grad_key, grad_value = lax.map(
        backward_one, (query_heads, key_heads, value_heads, log_sum, grad_heads, correction_heads)
    )
    return (
        attended,
        jnp.moveaxis(grad_query, 0, 1),
        jnp.moveaxis(grad_key, 0, 1),
        jnp.moveaxis(grad_value, 0, 1),
    )


def local(query_raw, key_raw, values, query_gain, key_gain, segment_ids, grad_attended):
    tok_rows = query_raw.shape[1]
    head_dim = query_gain.shape[0]
    query_heads = query_raw.shape[2] // head_dim
    key_heads = key_raw.shape[2] // head_dim
    group_size = query_heads // key_heads
    key_width = key_heads * head_dim
    query_unit, query_inverse = normalize(
        query_raw[0].astype(jnp.float32).reshape(tok_rows, query_heads, head_dim)
    )
    query_norm = (
        (query_unit * query_gain)
        .astype(jnp.bfloat16)
        .reshape(tok_rows, key_heads, group_size, head_dim)
    )
    key_unit, key_inverse = normalize(
        key_raw[0].astype(jnp.float32).reshape(tok_rows, key_heads, head_dim)
    )
    key_norm = (key_unit * key_gain).astype(jnp.bfloat16).reshape(tok_rows, key_width)
    own_rows = (key_norm, values[0], segment_ids[0] + 1)
    pieces = [own_rows]
    for distance in range(1, SPAN + 1):
        pieces.insert(0, shifted((own_rows[0], own_rows[1], own_rows[2]), "seq", distance))
    window = tuple(
        (jnp.concatenate([piece[member] for piece in pieces], axis=0) for member in range(3))
    )
    window_rows = (SPAN + 1) * tok_rows
    key_window = window[0].reshape(window_rows, key_heads, head_dim)
    value_window = window[1].reshape(window_rows, key_heads, head_dim)
    seg_window = window[2] - 1
    grad_out = grad_attended[0].reshape(tok_rows, key_heads, group_size, head_dim)
    attended, grad_query, grad_key, grad_value = device_block(
        query_norm, segment_ids[0], key_window, value_window, seg_window, grad_out
    )
    partial_value = jnp.concatenate(
        [grad_key.reshape(window_rows, key_width), grad_value.reshape(window_rows, key_width)],
        axis=1,
    )
    summed = partial_value[SPAN * tok_rows :]
    for distance in range(1, SPAN + 1):
        lower = (SPAN - distance) * tok_rows
        summed = summed + shifted(
            partial_value[lower : lower + tok_rows].astype(jnp.bfloat16), "seq", -distance
        ).astype(jnp.float32)
    grad_key_norm = summed[:, :key_width].reshape(tok_rows, key_heads, head_dim)
    grad_values = summed[:, key_width:].astype(jnp.bfloat16)
    grad_query = grad_query.reshape(tok_rows, query_heads, head_dim)
    grad_query_raw = norm_backward(grad_query, query_unit, query_inverse, query_gain).astype(
        jnp.bfloat16
    )
    grad_key_raw = norm_backward(grad_key_norm, key_unit, key_inverse, key_gain).astype(
        jnp.bfloat16
    )
    gain_totals = lax.psum(
        (
            jnp.sum(grad_query * query_unit, axis=(0, 1)),
            jnp.sum(grad_key_norm * key_unit, axis=(0, 1)),
        ),
        ("dp", "seq"),
    )
    return (
        attended.reshape(1, tok_rows, query_heads * head_dim),
        grad_query_raw.reshape(1, tok_rows, query_heads * head_dim),
        grad_key_raw.reshape(1, tok_rows, key_width),
        grad_values.reshape(1, tok_rows, key_width),
        gain_totals[0],
        gain_totals[1],
    )


def solution(mesh):
    return jax.shard_map(
        local,
        mesh=mesh,
        in_specs=(
            P("dp", "seq", None),
            P("dp", "seq", None),
            P("dp", "seq", None),
            P(),
            P(),
            P("dp", "seq"),
            P("dp", "seq", None),
        ),
        out_specs=(
            P("dp", "seq", None),
            P("dp", "seq", None),
            P("dp", "seq", None),
            P("dp", "seq", None),
            P(),
            P(),
        ),
        check_vma=False,
    )
```

profile of v0, /device:TPU:24, one launch (start us, length us, event | category | flops | bytes accessed | tf_op | source)
XLA Modules:
  0.0 563.2 jit_solution(9699735506927514874)
XLA Ops:
  4.6 13.1 %collective-permute-start.7 = (bf16[128,512]{1,0:T(8,128)(2,1)}, bf16[128,512]{1,0:T(8,128)(2,1)S(1)}, u32[]{:S(2)}, u32[]{:S(2)}) collective-permute-start(bf16[128,512]{1,0:T(8,128)(2,1)} %multiply_convert_fusion.3), channel_id=1, source_target_pairs={{0,7},{1,8},{2,9},{3,10},{4,11},{5,12},{6,13},{7,14},{8,15},{9,16}... | collective-permute-start | bytes 393224 | tf_op jit(solution)/shard_map/ppermute | solution.py:15
  17.7 7.3 %collective-permute-start.8 = (bf16[128,512]{1,0:T(8,128)(2,1)}, bf16[128,512]{1,0:T(8,128)(2,1)}, u32[]{:S(2)}, u32[]{:S(2)}) collective-permute-start(bf16[128,512]{1,0:T(8,128)(2,1)} %multiply_convert_fusion.3), channel_id=1, source_target_pairs={{0,6},{1,7},{2,8},{3,9},{4,10},{5,11},{6,12},{7,13},{8,14},{9,15},... | collective-permute-start | bytes 393224 | tf_op jit(solution)/shard_map/ppermute | solution.py:15
  37.9 38.3 %collective-permute-done = s32[128]{0:T(128)S(1)} collective-permute-done((s32[128]{0:T(128)S(1)}, s32[128]{0:T(128)S(1)}, u32[]{:S(2)}, u32[]{:S(2)}) %collective-permute-start) | collective-permute-done | bytes 544 | tf_op jit(solution)/shard_map/ppermute | solution.py:15
  76.2 13.2 %collective-permute-start.1 = (s32[128]{0:T(128)S(1)}, s32[128]{0:T(128)S(1)}, u32[]{:S(2)}, u32[]{:S(2)}) collective-permute-start(s32[128]{0:T(128)S(1)} %broadcast_add_fusion.1), channel_id=1, source_target_pairs={{0,6},{1,7},{2,8},{3,9},{4,10},{5,11},{6,12},{7,13},{8,14},{9,15},... | collective-permute-start | bytes 1544 | tf_op jit(solution)/shard_map/ppermute | solution.py:15
  89.4 5.9 %collective-permute-done.1 = s32[128]{0:T(128)S(1)} collective-permute-done((s32[128]{0:T(128)S(1)}, s32[128]{0:T(128)S(1)}, u32[]{:S(2)}, u32[]{:S(2)}) %collective-permute-start.1) | collective-permute-done | bytes 544 | tf_op jit(solution)/shard_map/ppermute | solution.py:15
  95.3 4.5 collective-permute-start.2
  99.8 7.8 %collective-permute-done.2 = s32[128]{0:T(128)S(1)} collective-permute-done((s32[128]{0:T(128)S(1)}, s32[128]{0:T(128)S(1)}, u32[]{:S(2)}, u32[]{:S(2)}) %collective-permute-start.2) | collective-permute-done | bytes 544 | tf_op jit(solution)/shard_map/ppermute | solution.py:15
  107.6 3.7 collective-permute-start.3
  111.3 6.5 %collective-permute-done.3 = s32[128]{0:T(128)S(1)} collective-permute-done((s32[128]{0:T(128)S(1)}, s32[128]{0:T(128)S(1)}, u32[]{:S(2)}, u32[]{:S(2)}) %collective-permute-start.3) | collective-permute-done | bytes 544 | tf_op jit(solution)/shard_map/ppermute | solution.py:15
  119.8 7.4 %collective-permute-done.4 = s32[128]{0:T(128)S(1)} collective-permute-done((s32[128]{0:T(128)S(1)}, s32[128]{0:T(128)S(1)}, u32[]{:S(2)}, u32[]{:S(2)}) %collective-permute-start.4) | collective-permute-done | bytes 544 | tf_op jit(solution)/shard_map/ppermute | solution.py:15
  129.1 6.5 %collective-permute-done.5 = s32[128]{0:T(128)S(1)} collective-permute-done((s32[128]{0:T(128)S(1)}, s32[128]{0:T(128)S(1)}, u32[]{:S(2)}, u32[]{:S(2)}) %collective-permute-start.5) | collective-permute-done | bytes 544 | tf_op jit(solution)/shard_map/ppermute | solution.py:15
  137.5 5.6 collective-permute-done.6
  151.5 10.9 %collective-permute-start.14 = (bf16[128,512]{0,1:T(8,128)(2,1)}, bf16[128,512]{0,1:T(8,128)(2,1)S(1)}, u32[]{:S(2)}, u32[]{:S(2)}) collective-permute-start(bf16[128,512]{0,1:T(8,128)(2,1)} %bitcast.266), channel_id=1, source_target_pairs={{0,7},{1,8},{2,9},{3,10},{4,11},{5,12},{6,13},{7,14},{8,15},{9,16}... | collective-permute-start | bytes 393224 | tf_op jit(solution)/shard_map/ppermute | solution.py:15
  170.2 20.2 %collective-permute-start.18 = (bf16[128,512]{0,1:T(8,128)(2,1)}, bf16[128,512]{0,1:T(8,128)(2,1)S(1)}, u32[]{:S(2)}, u32[]{:S(2)}) collective-permute-start(bf16[128,512]{0,1:T(8,128)(2,1)} %bitcast.270), channel_id=1, source_target_pairs={{0,3},{1,4},{2,5},{3,6},{4,7},{5,8},{6,9},{7,10},{8,11},{9,12},{10... | collective-permute-start | bytes 393224 | tf_op jit(solution)/shard_map/ppermute | solution.py:15
  191.4 13.3 %collective-permute-start.19 = (bf16[128,512]{0,1:T(8,128)(2,1)}, bf16[128,512]{0,1:T(8,128)(2,1)S(1)}, u32[]{:S(2)}, u32[]{:S(2)}) collective-permute-start(bf16[128,512]{0,1:T(8,128)(2,1)} %bitcast.271), channel_id=1, source_target_pairs={{0,2},{1,3},{2,4},{3,5},{4,6},{5,7},{6,8},{7,9},{8,10},{9,11},{10,... | collective-permute-start | bytes 393224 | tf_op jit(solution)/shard_map/ppermute | solution.py:15
  207.3 12.4 %collective-permute-start.20 = (bf16[128,512]{0,1:T(8,128)(2,1)}, bf16[128,512]{0,1:T(8,128)(2,1)S(1)}, u32[]{:S(2)}, u32[]{:S(2)}) collective-permute-start(bf16[128,512]{0,1:T(8,128)(2,1)} %bitcast.272), channel_id=1, source_target_pairs={{0,1},{1,2},{2,3},{3,4},{4,5},{5,6},{6,7},{7,8},{8,9},{9,10},{10,1... | collective-permute-start | bytes 393224 | tf_op jit(solution)/shard_map/ppermute | solution.py:15
  220.4 6.2 %collective-permute-done.16 = bf16[128,512]{0,1:T(8,128)(2,1)S(1)} collective-permute-done((bf16[128,512]{0,1:T(8,128)(2,1)}, bf16[128,512]{0,1:T(8,128)(2,1)S(1)}, u32[]{:S(2)}, u32[]{:S(2)}) %collective-permute-start.16) | collective-permute-done | bytes 131104 | tf_op jit(solution)/shard_map/ppermute | solution.py:15
  227.9 5.1 collective-permute-done.18
  233.7 3.4 collective-permute-done.19
  241.5 16.0 %while.30 = (s32[]{:T(128)}, bf16[4,128,5,128]{1,3,2,0:T(8,128)(2,1)S(1)}, f32[4,128,5]{1,2,0:T(8,128)}, bf16[4,128,5,128]{3,1,2,0:T(8,128)(2,1)S(1)}, bf16[4,10...) while((s32[]{:T(128)}, ...), condition=%wide.region_5.6_spmd.clone.clone, body=%wide.region_2.5_spmd.clone.sunk.clone | while | flops 343145856 | bytes 9439325 | solution.py:77
  259.4 31.6 %while.31 = (s32[]{:T(128)}, f32[4,128,5,128]{1,3,2,0:T(8,128)}, f32[4,1024,128]{2,1,0:T(8,128)}, f32[4,1024,128]{2,1,0:T(8,128)}, bf16[4,128,5,128]{3,1,2,0:T(8...) while((s32[]{:T(128)}, f32[4,128,5,128]{1,3,2,0:T(8,128)}, ...), condition=%wide.region_8.9_spmd.clone.clone, body=%wide.region_7.8_spmd.clone.sunk.clone | while | flops 846462976 | bytes 17665692 | solution.py:88
  298.0 3.3 collective-permute-start.21
  301.3 3.4 collective-permute-start.22
  307.3 4.0 collective-permute-start.24
  311.3 6.4 %collective-permute-start.25 = (bf16[128,1024]{1,0:T(8,128)(2,1)}, bf16[128,1024]{1,0:T(8,128)(2,1)}, u32[]{:S(2)}, u32[]{:S(2)}) collective-permute-start(bf16[128,1024]{1,0:T(8,128)(2,1)} %get-tuple-element.361), channel_id=1, source_target_pairs={{5,0},{6,1},{7,2},{8,3},{9,4},{10,5},{11,6},{12,7},{13,8},{14,9},{... | collective-permute-start | bytes 786440 | tf_op jit(solution)/shard_map/ppermute | solution.py:15
  317.7 6.4 %collective-permute-start.26 = (bf16[128,1024]{1,0:T(8,128)(2,1)}, bf16[128,1024]{1,0:T(8,128)(2,1)}, u32[]{:S(2)}, u32[]{:S(2)}) collective-permute-start(bf16[128,1024]{1,0:T(8,128)(2,1)} %get-tuple-element.360), channel_id=1, source_target_pairs={{6,0},{7,1},{8,2},{9,3},{10,4},{11,5},{12,6},{13,7},{14,8},{15,9},... | collective-permute-start | bytes 786440 | tf_op jit(solution)/shard_map/ppermute | solution.py:15
  324.1 11.8 %collective-permute-done.22 = bf16[128,1024]{1,0:T(8,128)(2,1)} collective-permute-done((bf16[128,1024]{1,0:T(8,128)(2,1)}, bf16[128,1024]{1,0:T(8,128)(2,1)}, u32[]{:S(2)}, u32[]{:S(2)}) %collective-permute-start.22) | collective-permute-done | bytes 262176 | tf_op jit(solution)/shard_map/ppermute | solution.py:15
  343.7 17.3 %collective-permute-done.23 = bf16[128,1024]{1,0:T(8,128)(2,1)} collective-permute-done((bf16[128,1024]{1,0:T(8,128)(2,1)}, bf16[128,1024]{1,0:T(8,128)(2,1)}, u32[]{:S(2)}, u32[]{:S(2)}) %collective-permute-start.23) | collective-permute-done | bytes 262176 | tf_op jit(solution)/shard_map/ppermute | solution.py:15
  360.9 13.0 %collective-permute-done.24 = bf16[128,1024]{1,0:T(8,128)(2,1)} collective-permute-done((bf16[128,1024]{1,0:T(8,128)(2,1)}, bf16[128,1024]{1,0:T(8,128)(2,1)}, u32[]{:S(2)}, u32[]{:S(2)}) %collective-permute-start.24) | collective-permute-done | bytes 262176 | tf_op jit(solution)/shard_map/ppermute | solution.py:15
  374.0 31.3 %collective-permute-done.25 = bf16[128,1024]{1,0:T(8,128)(2,1)} collective-permute-done((bf16[128,1024]{1,0:T(8,128)(2,1)}, bf16[128,1024]{1,0:T(8,128)(2,1)}, u32[]{:S(2)}, u32[]{:S(2)}) %collective-permute-start.25) | collective-permute-done | bytes 262176 | tf_op jit(solution)/shard_map/ppermute | solution.py:15
  405.2 34.9 %collective-permute-done.26 = bf16[128,1024]{1,0:T(8,128)(2,1)} collective-permute-done((bf16[128,1024]{1,0:T(8,128)(2,1)}, bf16[128,1024]{1,0:T(8,128)(2,1)}, u32[]{:S(2)}, u32[]{:S(2)}) %collective-permute-start.26) | collective-permute-done | bytes 262176 | tf_op jit(solution)/shard_map/ppermute | solution.py:15
  443.5 119.0 %all-reduce = (f32[128]{0:T(128)}, f32[128]{0:T(128)}) all-reduce(f32[128]{0:T(128)S(1)} %get-tuple-element.302, f32[128]{0:T(128)S(1)} %bitcast_reduce_fusion), channel_id=1, replica_groups=mesh['dp'=8,'seq'=64] {'dp','seq'}, use_global_device_ids=true, to_apply=%region_12.13 | all-reduce | flops 256 | bytes 2048 | tf_op jit(solution)/shard_map/psum | solution.py:152
  (190 shorter events, 119.6 us)
Async XLA Ops:
  4.6 140.5 %collective-permute-start.7 = (bf16[128,512]{1,0:T(8,128)(2,1)}, bf16[128,512]{1,0:T(8,128)(2,1)S(1)}, u32[]{:S(2)}, u32[]{:S(2)}) collective-permute-start(bf16[128,512]{1,0:T(8,128)(2,1)} %multiply_convert_fusion.3), channel_id=1, source_target_pairs={{0,7},{1,8},{2,9},{3,10},{4,11},{5,12},{6,13},{7,14},{8,15},{9,16}... | collective-permute-start | bytes 393224 | tf_op jit(solution)/shard_map/ppermute | solution.py:15
  17.7 130.9 %collective-permute-start.8 = (bf16[128,512]{1,0:T(8,128)(2,1)}, bf16[128,512]{1,0:T(8,128)(2,1)}, u32[]{:S(2)}, u32[]{:S(2)}) collective-permute-start(bf16[128,512]{1,0:T(8,128)(2,1)} %multiply_convert_fusion.3), channel_id=1, source_target_pairs={{0,6},{1,7},{2,8},{3,9},{4,10},{5,11},{6,12},{7,13},{8,14},{9,15},... | collective-permute-start | bytes 393224 | tf_op jit(solution)/shard_map/ppermute | solution.py:15
  25.1 126.5 %collective-permute-start.9 = (bf16[128,512]{1,0:T(8,128)(2,1)}, bf16[128,512]{1,0:T(8,128)(2,1)}, u32[]{:S(2)}, u32[]{:S(2)}) collective-permute-start(bf16[128,512]{1,0:T(8,128)(2,1)} %multiply_convert_fusion.3), channel_id=1, source_target_pairs={{0,5},{1,6},{2,7},{3,8},{4,9},{5,10},{6,11},{7,12},{8,13},{9,14},{... | collective-permute-start | bytes 393224 | tf_op jit(solution)/shard_map/ppermute | solution.py:15
  27.0 136.4 %collective-permute-start.10 = (bf16[128,512]{1,0:T(8,128)(2,1)}, bf16[128,512]{1,0:T(8,128)(2,1)}, u32[]{:S(2)}, u32[]{:S(2)}) collective-permute-start(bf16[128,512]{1,0:T(8,128)(2,1)} %multiply_convert_fusion.3), channel_id=1, source_target_pairs={{0,4},{1,5},{2,6},{3,7},{4,8},{5,9},{6,10},{7,11},{8,12},{9,13},{1... | collective-permute-start | bytes 393224 | tf_op jit(solution)/shard_map/ppermute | solution.py:15
  30.4 45.8 %collective-permute-start = (s32[128]{0:T(128)S(1)}, s32[128]{0:T(128)S(1)}, u32[]{:S(2)}, u32[]{:S(2)}) collective-permute-start(s32[128]{0:T(128)S(1)} %broadcast_add_fusion.1), channel_id=1, source_target_pairs={{0,7},{1,8},{2,9},{3,10},{4,11},{5,12},{6,13},{7,14},{8,15},{9,16}... | collective-permute-start | bytes 1544 | tf_op jit(solution)/shard_map/ppermute | solution.py:15
  34.6 110.5 %copy-start.12 = (s32[1,128]{1,0:T(1,128)S(1)}, s32[1,128]{1,0:T(1,128)}, u32[]{:S(2)}) copy-start(s32[1,128]{1,0:T(1,128)} %param.16) | copy-start | bytes 1540
  37.9 200.7 %copy-start.5 = (bf16[1,128,512]{1,2,0:T(8,128)(2,1)S(1)}, bf16[1,128,512]{1,2,0:T(8,128)(2,1)}, u32[]{:S(2)}) copy-start(bf16[1,128,512]{1,2,0:T(8,128)(2,1)} %copy.166) | copy-start | bytes 393220
  76.2 19.1 %collective-permute-start.1 = (s32[128]{0:T(128)S(1)}, s32[128]{0:T(128)S(1)}, u32[]{:S(2)}, u32[]{:S(2)}) collective-permute-start(s32[128]{0:T(128)S(1)} %broadcast_add_fusion.1), channel_id=1, source_target_pairs={{0,6},{1,7},{2,8},{3,9},{4,10},{5,11},{6,12},{7,13},{8,14},{9,15},... | collective-permute-start | bytes 1544 | tf_op jit(solution)/shard_map/ppermute | solution.py:15
  95.3 12.3 %collective-permute-start.2 = (s32[128]{0:T(128)S(1)}, s32[128]{0:T(128)S(1)}, u32[]{:S(2)}, u32[]{:S(2)}) collective-permute-start(s32[128]{0:T(128)S(1)} %broadcast_add_fusion.1), channel_id=1, source_target_pairs={{0,5},{1,6},{2,7},{3,8},{4,9},{5,10},{6,11},{7,12},{8,13},{9,14},{... | collective-permute-start | bytes 1544 | tf_op jit(solution)/shard_map/ppermute | solution.py:15
  107.6 10.2 %collective-permute-start.3 = (s32[128]{0:T(128)S(1)}, s32[128]{0:T(128)S(1)}, u32[]{:S(2)}, u32[]{:S(2)}) collective-permute-start(s32[128]{0:T(128)S(1)} %broadcast_add_fusion.1), channel_id=1, source_target_pairs={{0,4},{1,5},{2,6},{3,7},{4,8},{5,9},{6,10},{7,11},{8,12},{9,13},{1... | collective-permute-start | bytes 1544 | tf_op jit(solution)/shard_map/ppermute | solution.py:15
  117.9 9.3 %collective-permute-start.4 = (s32[128]{0:T(128)S(1)}, s32[128]{0:T(128)S(1)}, u32[]{:S(2)}, u32[]{:S(2)}) collective-permute-start(s32[128]{0:T(128)S(1)} %broadcast_add_fusion.1), channel_id=1, source_target_pairs={{0,3},{1,4},{2,5},{3,6},{4,7},{5,8},{6,9},{7,10},{8,11},{9,12},{10... | collective-permute-start | bytes 1544 | tf_op jit(solution)/shard_map/ppermute | solution.py:15
  127.2 8.4 %collective-permute-start.5 = (s32[128]{0:T(128)S(1)}, s32[128]{0:T(128)S(1)}, u32[]{:S(2)}, u32[]{:S(2)}) collective-permute-start(s32[128]{0:T(128)S(1)} %broadcast_add_fusion.1), channel_id=1, source_target_pairs={{0,2},{1,3},{2,4},{3,5},{4,6},{5,7},{6,8},{7,9},{8,10},{9,11},{10,... | collective-permute-start | bytes 1544 | tf_op jit(solution)/shard_map/ppermute | solution.py:15
  135.6 7.5 %collective-permute-start.6 = (s32[128]{0:T(128)S(1)}, s32[128]{0:T(128)S(1)}, u32[]{:S(2)}, u32[]{:S(2)}) collective-permute-start(s32[128]{0:T(128)S(1)} %broadcast_add_fusion.1), channel_id=1, source_target_pairs={{0,1},{1,2},{2,3},{3,4},{4,5},{5,6},{6,7},{7,8},{8,9},{9,10},{10,1... | collective-permute-start | bytes 1544 | tf_op jit(solution)/shard_map/ppermute | solution.py:15
  143.2 23.1 %collective-permute-start.11 = (bf16[128,512]{1,0:T(8,128)(2,1)}, bf16[128,512]{1,0:T(8,128)(2,1)S(1)}, u32[]{:S(2)}, u32[]{:S(2)}) collective-permute-start(bf16[128,512]{1,0:T(8,128)(2,1)} %multiply_convert_fusion.3), channel_id=1, source_target_pairs={{0,3},{1,4},{2,5},{3,6},{4,7},{5,8},{6,9},{7,10},{8,11},{9,12},{10... | collective-permute-start | bytes 393224 | tf_op jit(solution)/shard_map/ppermute | solution.py:15
  145.8 22.5 %collective-permute-start.12 = (bf16[128,512]{1,0:T(8,128)(2,1)}, bf16[128,512]{1,0:T(8,128)(2,1)S(1)}, u32[]{:S(2)}, u32[]{:S(2)}) collective-permute-start(bf16[128,512]{1,0:T(8,128)(2,1)} %multiply_convert_fusion.3), channel_id=1, source_target_pairs={{0,2},{1,3},{2,4},{3,5},{4,6},{5,7},{6,8},{7,9},{8,10},{9,11},{10,... | collective-permute-start | bytes 393224 | tf_op jit(solution)/shard_map/ppermute | solution.py:15
  148.6 21.6 %collective-permute-start.13 = (bf16[128,512]{1,0:T(8,128)(2,1)}, bf16[128,512]{1,0:T(8,128)(2,1)S(1)}, u32[]{:S(2)}, u32[]{:S(2)}) collective-permute-start(bf16[128,512]{1,0:T(8,128)(2,1)} %multiply_convert_fusion.3), channel_id=1, source_target_pairs={{0,1},{1,2},{2,3},{3,4},{4,5},{5,6},{6,7},{7,8},{8,9},{9,10},{10,1... | collective-permute-start | bytes 393224 | tf_op jit(solution)/shard_map/ppermute | solution.py:15
  151.5 39.8 %collective-permute-start.14 = (bf16[128,512]{0,1:T(8,128)(2,1)}, bf16[128,512]{0,1:T(8,128)(2,1)S(1)}, u32[]{:S(2)}, u32[]{:S(2)}) collective-permute-start(bf16[128,512]{0,1:T(8,128)(2,1)} %bitcast.266), channel_id=1, source_target_pairs={{0,7},{1,8},{2,9},{3,10},{4,11},{5,12},{6,13},{7,14},{8,15},{9,16}... | collective-permute-start | bytes 393224 | tf_op jit(solution)/shard_map/ppermute | solution.py:15
  163.4 43.9 %collective-permute-start.15 = (bf16[128,512]{0,1:T(8,128)(2,1)}, bf16[128,512]{0,1:T(8,128)(2,1)S(1)}, u32[]{:S(2)}, u32[]{:S(2)}) collective-permute-start(bf16[128,512]{0,1:T(8,128)(2,1)} %bitcast.267), channel_id=1, source_target_pairs={{0,6},{1,7},{2,8},{3,9},{4,10},{5,11},{6,12},{7,13},{8,14},{9,15},... | collective-permute-start | bytes 393224 | tf_op jit(solution)/shard_map/ppermute | solution.py:15
  166.3 60.3 %collective-permute-start.16 = (bf16[128,512]{0,1:T(8,128)(2,1)}, bf16[128,512]{0,1:T(8,128)(2,1)S(1)}, u32[]{:S(2)}, u32[]{:S(2)}) collective-permute-start(bf16[128,512]{0,1:T(8,128)(2,1)} %bitcast.268), channel_id=1, source_target_pairs={{0,5},{1,6},{2,7},{3,8},{4,9},{5,10},{6,11},{7,12},{8,13},{9,14},{... | collective-permute-start | bytes 393224 | tf_op jit(solution)/shard_map/ppermute | solution.py:15
  168.3 59.0 %collective-permute-start.17 = (bf16[128,512]{0,1:T(8,128)(2,1)}, bf16[128,512]{0,1:T(8,128)(2,1)S(1)}, u32[]{:S(2)}, u32[]{:S(2)}) collective-permute-start(bf16[128,512]{0,1:T(8,128)(2,1)} %bitcast.269), channel_id=1, source_target_pairs={{0,4},{1,5},{2,6},{3,7},{4,8},{5,9},{6,10},{7,11},{8,12},{9,13},{1... | collective-permute-start | bytes 393224 | tf_op jit(solution)/shard_map/ppermute | solution.py:15
  170.2 62.8 %collective-permute-start.18 = (bf16[128,512]{0,1:T(8,128)(2,1)}, bf16[128,512]{0,1:T(8,128)(2,1)S(1)}, u32[]{:S(2)}, u32[]{:S(2)}) collective-permute-start(bf16[128,512]{0,1:T(8,128)(2,1)} %bitcast.270), channel_id=1, source_target_pairs={{0,3},{1,4},{2,5},{3,6},{4,7},{5,8},{6,9},{7,10},{8,11},{9,12},{10... | collective-permute-start | bytes 393224 | tf_op jit(solution)/shard_map/ppermute | solution.py:15
  191.4 45.8 %collective-permute-start.19 = (bf16[128,512]{0,1:T(8,128)(2,1)}, bf16[128,512]{0,1:T(8,128)(2,1)S(1)}, u32[]{:S(2)}, u32[]{:S(2)}) collective-permute-start(bf16[128,512]{0,1:T(8,128)(2,1)} %bitcast.271), channel_id=1, source_target_pairs={{0,2},{1,3},{2,4},{3,5},{4,6},{5,7},{6,8},{7,9},{8,10},{9,11},{10,... | collective-permute-start | bytes 393224 | tf_op jit(solution)/shard_map/ppermute | solution.py:15
  207.3 30.6 %collective-permute-start.20 = (bf16[128,512]{0,1:T(8,128)(2,1)}, bf16[128,512]{0,1:T(8,128)(2,1)S(1)}, u32[]{:S(2)}, u32[]{:S(2)}) collective-permute-start(bf16[128,512]{0,1:T(8,128)(2,1)} %bitcast.272), channel_id=1, source_target_pairs={{0,1},{1,2},{2,3},{3,4},{4,5},{5,6},{6,7},{7,8},{8,9},{9,10},{10,1... | collective-permute-start | bytes 393224 | tf_op jit(solution)/shard_map/ppermute | solution.py:15
  298.0 19.7 %collective-permute-start.21 = (bf16[128,1024]{1,0:T(8,128)(2,1)}, bf16[128,1024]{1,0:T(8,128)(2,1)}, u32[]{:S(2)}, u32[]{:S(2)}) collective-permute-start(bf16[128,1024]{1,0:T(8,128)(2,1)} %get-tuple-element.358), channel_id=1, source_target_pairs={{1,0},{2,1},{3,2},{4,3},{5,4},{6,5},{7,6},{8,7},{9,8},{10,9},{11,1... | collective-permute-start | bytes 786440 | tf_op jit(solution)/shard_map/ppermute | solution.py:15
  301.3 34.7 %collective-permute-start.22 = (bf16[128,1024]{1,0:T(8,128)(2,1)}, bf16[128,1024]{1,0:T(8,128)(2,1)}, u32[]{:S(2)}, u32[]{:S(2)}) collective-permute-start(bf16[128,1024]{1,0:T(8,128)(2,1)} %get-tuple-element.364), channel_id=1, source_target_pairs={{2,0},{3,1},{4,2},{5,3},{6,4},{7,5},{8,6},{9,7},{10,8},{11,9},{12,... | collective-permute-start | bytes 786440 | tf_op jit(solution)/shard_map/ppermute | solution.py:15
  304.8 56.2 %collective-permute-start.23 = (bf16[128,1024]{1,0:T(8,128)(2,1)}, bf16[128,1024]{1,0:T(8,128)(2,1)}, u32[]{:S(2)}, u32[]{:S(2)}) collective-permute-start(bf16[128,1024]{1,0:T(8,128)(2,1)} %get-tuple-element.363), channel_id=1, source_target_pairs={{3,0},{4,1},{5,2},{6,3},{7,4},{8,5},{9,6},{10,7},{11,8},{12,9},{13... | collective-permute-start | bytes 786440 | tf_op jit(solution)/shard_map/ppermute | solution.py:15
  307.3 66.7 %collective-permute-start.24 = (bf16[128,1024]{1,0:T(8,128)(2,1)}, bf16[128,1024]{1,0:T(8,128)(2,1)}, u32[]{:S(2)}, u32[]{:S(2)}) collective-permute-start(bf16[128,1024]{1,0:T(8,128)(2,1)} %get-tuple-element.362), channel_id=1, source_target_pairs={{4,0},{5,1},{6,2},{7,3},{8,4},{9,5},{10,6},{11,7},{12,8},{13,9},{1... | collective-permute-start | bytes 786440 | tf_op jit(solution)/shard_map/ppermute | solution.py:15
  311.3 93.9 %collective-permute-start.25 = (bf16[128,1024]{1,0:T(8,128)(2,1)}, bf16[128,1024]{1,0:T(8,128)(2,1)}, u32[]{:S(2)}, u32[]{:S(2)}) collective-permute-start(bf16[128,1024]{1,0:T(8,128)(2,1)} %get-tuple-element.361), channel_id=1, source_target_pairs={{5,0},{6,1},{7,2},{8,3},{9,4},{10,5},{11,6},{12,7},{13,8},{14,9},{... | collective-permute-start | bytes 786440 | tf_op jit(solution)/shard_map/ppermute | solution.py:15
  317.7 122.4 %collective-permute-start.26 = (bf16[128,1024]{1,0:T(8,128)(2,1)}, bf16[128,1024]{1,0:T(8,128)(2,1)}, u32[]{:S(2)}, u32[]{:S(2)}) collective-permute-start(bf16[128,1024]{1,0:T(8,128)(2,1)} %get-tuple-element.360), channel_id=1, source_target_pairs={{6,0},{7,1},{8,2},{9,3},{10,4},{11,5},{12,6},{13,7},{14,8},{15,9},... | collective-permute-start | bytes 786440 | tf_op jit(solution)/shard_map/ppermute | solution.py:15
  335.9 104.2 %collective-permute-start.27 = (bf16[128,1024]{1,0:T(8,128)(2,1)}, bf16[128,1024]{1,0:T(8,128)(2,1)}, u32[]{:S(2)}, u32[]{:S(2)}) collective-permute-start(bf16[128,1024]{1,0:T(8,128)(2,1)} %get-tuple-element.359), channel_id=1, source_target_pairs={{7,0},{8,1},{9,2},{10,3},{11,4},{12,5},{13,6},{14,7},{15,8},{16,9}... | collective-permute-start | bytes 786440 | tf_op jit(solution)/shard_map/ppermute | solution.py:15
  342.6 99.4 %copy-start.3 = (bf16[1,128,512]{2,1,0:T(8,128)(2,1)S(1)}, bf16[1,128,512]{2,1,0:T(8,128)(2,1)}, u32[]{:S(2)}) copy-start(bf16[1,128,512]{2,1,0:T(8,128)(2,1)} %param.12) | copy-start | bytes 393220
  343.7 218.8 %copy-start.14 = (f32[512]{0:T(512)S(1)}, f32[512]{0:T(512)}, u32[]{:S(2)}) copy-start(f32[512]{0:T(512)} %copy-done.13) | copy-start | bytes 6148
  (17 other events, 308.0 us)
where the time goes:
time: 568 us; the launch traced here: 563 us
  waiting for transfers between devices  203 us (36%)
  starting transfers between devices  150 us (26%)
  blocking collectives  119 us (21%)
  matrix products  38.1 us (7%)
  local copies, waits for them, and re-layouts  30.9 us (5%)
  other arithmetic  20.2 us (4%)
    ppermute x28, waiting for transfers between devices, shifted(): lax.ppermute(value, axis, [(source, source + steps) for source in range(i...  203 us
    ppermute x28, starting transfers between devices, shifted(): lax.ppermute(value, axis, [(source, source + steps) for source in range(i...  150 us
    psum x1, blocking collectives, local(): lax.psum((jnp.sum(grad_query * query_unit, axis=(0, 1)), jnp.sum(grad_key...  119 us
    unnamed x64, local copies, waits for them, and re-layouts  21.1 us
  transfers between devices with their start and end apart: 28, of which 16 were waited for; matrix products, arithmetic and copies ran while one was open for 4% of the time, Pallas kernels for 0%

commit v1 on v0

v1 whole, which is shorter than its diff:
```python
import math

import jax
import jax.numpy as jnp
from jax import lax
from jax.experimental import pallas as pl
from jax.experimental.pallas import tpu as pltpu
from jax.sharding import PartitionSpec as P

SPAN = 7
BLOCKS = SPAN + 1
HEAD = 128
TOK = 128
KV = 4
GROUP = 5
WIDTH = GROUP * TOK
STAGGER = 2
ROUNDS = (KV - 1) * STAGGER + 2 * SPAN + 1
EPSILON = 1e-06
SCALE = HEAD**-0.5
MESH = pl.DeviceIdType.MESH

NT = (((1,), (1,)), ((), ()))
NN = (((1,), (0,)), ((), ()))
TN = (((0,), (0,)), ((), ()))


def dot(a, b, dims):
    return lax.dot_general(a, b, dims, preferred_element_type=jnp.float32)


def normalize(rows):
    inverse = lax.rsqrt(jnp.mean(rows * rows, axis=-1, keepdims=True) + EPSILON)
    return rows * inverse, inverse


def norm_backward(grad, unit, inverse, gain):
    scaled = grad * gain
    return inverse * (scaled - unit * jnp.mean(scaled * unit, axis=-1, keepdims=True))


def lanes(head):
    return pl.ds(pl.multiple_of(head * HEAD, HEAD), HEAD)


def kernel(
    query_ref, key_ref, value_ref, query_gain_ref, key_gain_ref, segment_ref, grad_ref,
    attended_ref, grad_query_ref, grad_key_ref, grad_value_ref, gains_ref,
    window, ids, bias, query_norm, grad_rows, grad_cols, key_norm, key_unit, scores, row_max,
    weights, grad_scores, partial, outgoing, incoming,
    up_send, up_recv, id_send, id_recv, down_send, down_recv,
):
    count = lax.axis_size("seq")
    me = lax.axis_index("seq")
    dp = lax.axis_index("dp")
    after = lax.rem(me + 1, count)
    before = lax.rem(me + count - 1, count)

    barrier = pltpu.get_barrier_semaphore()
    for neighbour in (after, before):
        pl.semaphore_signal(barrier, inc=1, device_id=(dp, neighbour), device_id_type=MESH)

    def up(head, step):
        return pltpu.make_async_remote_copy(
            src_ref=window.at[head, step],
            dst_ref=window.at[head, step + 1],
            send_sem=up_send.at[head, step],
            recv_sem=up_recv.at[head, step],
            device_id=(dp, after),
            device_id_type=MESH,
        )

    def up_ids(step):
        return pltpu.make_async_remote_copy(
            src_ref=ids.at[step],
            dst_ref=ids.at[step + 1],
            send_sem=id_send.at[step],
            recv_sem=id_recv.at[step],
            device_id=(dp, after),
            device_id_type=MESH,
        )

    def down(head, step):
        return pltpu.make_async_remote_copy(
            src_ref=outgoing.at[head, step],
            dst_ref=incoming.at[head, step],
            send_sem=down_send.at[head, step],
            recv_sem=down_recv.at[head, step],
            device_id=(dp, before),
            device_id_type=MESH,
        )

    own_ids = segment_ref[...].astype(jnp.float32)
    ids[0] = jnp.broadcast_to(own_ids, (16, TOK)).astype(jnp.bfloat16)
    for head in range(KV):
        at = slice(head * HEAD, (head + 1) * HEAD)
        window[head, 0, :TOK] = key_ref[:, at]
        window[head, 0, TOK:] = value_ref[:, at]
    pl.semaphore_wait(barrier, 2)

    def prepare(head):
        group, member = head // GROUP, lax.rem(head, GROUP)
        rows = pl.ds(pl.multiple_of(member * TOK, TOK), TOK)
        unit, _ = normalize(query_ref[:, lanes(head)].astype(jnp.float32))
        query_norm[group, rows, :] = (unit * query_gain_ref[...]).astype(jnp.bfloat16)
        grad = grad_ref[:, lanes(head)]
        grad_rows[group, rows, :] = grad
        grad_cols[group, :, rows] = grad.astype(jnp.float32).T.astype(jnp.bfloat16)

    def mask_block(step):
        key_ids = jnp.broadcast_to(ids[step, 0:16, :].astype(jnp.float32)[0:1], (TOK, TOK)).T
        seen = key_ids == own_ids
        key_at = lax.broadcasted_iota(jnp.int32, (TOK, TOK), 0)
        query_at = lax.broadcasted_iota(jnp.int32, (TOK, TOK), 1)
        seen = seen & (key_at <= query_at + jnp.where(step > 0, TOK, 0))
        bias[step] = jnp.where(seen, 0.0, -1e30)

    def score_block(head, step):
        unit, _ = normalize(window[head, step, :TOK].astype(jnp.float32))
        key_unit[head, step] = unit
        keys = (unit * key_gain_ref[...]).astype(jnp.bfloat16)
        key_norm[head, step] = keys
        raw = dot(keys, query_norm[head], NT) * (SCALE * math.log2(math.e))
        block_bias = bias[step]
        for member in range(GROUP):
            at = slice(member * TOK, (member + 1) * TOK)
            part = raw[:, at] + block_bias
            scores[head, step, :, at] = part
            top = jnp.max(part.reshape(TOK // 8, 8, TOK), axis=0)
            row_max[head, :, at] = jnp.maximum(row_max[head, :, at], top)

    def head_work(head):
        top = jnp.max(row_max[head], axis=0, keepdims=True)

        def exponent(step, total):
            part = jnp.exp2(scores[head, step] - top)
            scores[head, step] = part
            return total + jnp.sum(part.reshape(TOK // 8, 8, WIDTH), axis=0)

        total = lax.fori_loop(0, BLOCKS, exponent, jnp.zeros((8, WIDTH), jnp.float32))
        inverse = 1.0 / jnp.sum(total, axis=0, keepdims=True)

        def weigh(step, _):
            weights[step] = (scores[head, step] * inverse).astype(jnp.bfloat16)
            partial[head, step, TOK:] = dot(weights[step], grad_rows[head], NN)
            return 0

        lax.fori_loop(0, BLOCKS, weigh, 0)
        value_rows = window[head, :, TOK:, :].reshape(BLOCKS * TOK, HEAD)
        output = dot(value_rows, weights[...].reshape(BLOCKS * TOK, WIDTH), TN)
        output = output.astype(jnp.bfloat16).astype(jnp.float32)
        correction = jnp.sum(output * grad_cols[head].astype(jnp.float32), axis=0, keepdims=True)
        for member in range(GROUP):
            at = slice(member * TOK, (member + 1) * TOK)
            attended_ref[:, lanes(head * GROUP + member)] = output[:, at].T.astype(jnp.bfloat16)
        scaled = inverse * SCALE

        def grad_block(step, _):
            grad_prob = dot(window[head, step, TOK:], grad_rows[head], NT)
            grad_scores[step] = (
                (scores[head, step] * scaled) * (grad_prob - correction)
            ).astype(jnp.bfloat16)
            grad_key = dot(grad_scores[step], query_norm[head], NN)
            partial[head, step, :TOK] = grad_key
            gains_ref[8:] += jnp.sum(
                (grad_key * key_unit[head, step]).reshape(TOK // 8, 8, HEAD), axis=0
            )
            return 0

        lax.fori_loop(0, BLOCKS, grad_block, 0)
        outgoing[head, 0] = partial[head, SPAN].astype(jnp.bfloat16)
        down(head, 0).start()

        key_rows = key_norm[head].reshape(BLOCKS * TOK, HEAD)
        grad_query = dot(key_rows, grad_scores[...].reshape(BLOCKS * TOK, WIDTH), TN)
        for member in range(GROUP):
            at = slice(member * TOK, (member + 1) * TOK)
            where = lanes(head * GROUP + member)
            unit, query_inverse = normalize(query_ref[:, where].astype(jnp.float32))
            grad = grad_query[:, at].T
            gains_ref[:8] += jnp.sum((grad * unit).reshape(TOK // 8, 8, HEAD), axis=0)
            grad_query_ref[:, where] = norm_backward(
                grad, unit, query_inverse, query_gain_ref[...]
            ).astype(jnp.bfloat16)

    def receive(head, step):
        @pl.when((step >= 1) & (step <= SPAN))
        def _():
            up(head, step - 1).wait_recv()

            @pl.when(head == 0)
            def _():
                up_ids(step - 1).wait_recv()

        @pl.when((step >= 0) & (step < SPAN))
        def _():
            up(head, step).start()

            @pl.when(head == 0)
            def _():
                up_ids(step).start()

        back = step - SPAN

        @pl.when((back >= 1) & (back <= SPAN))
        def _():
            down(head, back - 1).wait_recv()
            total = incoming[head, back - 1].astype(jnp.float32) + partial[head, SPAN - back]

            @pl.when(back < SPAN)
            def _():
                outgoing[head, back] = total.astype(jnp.bfloat16)
                down(head, back).start()

            @pl.when(back == SPAN)
            def _():
                at = lanes(head)
                unit, inverse = normalize(key_ref[:, at].astype(jnp.float32))
                grad_key_ref[:, at] = norm_backward(
                    total[:TOK], unit, inverse, key_gain_ref[...]
                ).astype(jnp.bfloat16)
                grad_value_ref[:, at] = total[TOK:].astype(jnp.bfloat16)

    def work(head, step):
        @pl.when(step == 0)
        def _():
            def one(member, carry):
                prepare(head * GROUP + member)
                return carry

            lax.fori_loop(0, GROUP, one, 0)

        @pl.when((step >= 0) & (step <= SPAN))
        def _():
            @pl.when(head == 0)
            def _():
                mask_block(step)

            score_block(head, step)

        @pl.when(step == SPAN)
        def _():
            head_work(head)

    row_max[...] = jnp.full(row_max.shape, -jnp.inf, jnp.float32)
    gains_ref[...] = jnp.zeros(gains_ref.shape, jnp.float32)

    def one_round(index, carry):
        def first(head, inner):
            receive(head, index - STAGGER * head)
            return inner

        def second(head, inner):
            work(head, index - STAGGER * head)
            return inner

        lax.fori_loop(0, KV, first, 0)
        lax.fori_loop(0, KV, second, 0)
        return carry

    lax.fori_loop(0, ROUNDS, one_round, 0)

    def drain(head, carry):
        def one(step, inner):
            up(head, step).wait_send()
            down(head, step).wait_send()

            @pl.when(head == 0)
            def _():
                up_ids(step).wait_send()

            return inner

        return lax.fori_loop(0, SPAN, one, carry)

    lax.fori_loop(0, KV, drain, 0)


def local(query_raw, key_raw, values, query_gain, key_gain, segment_ids, grad_attended):
    wide, narrow = (TOK, KV * GROUP * HEAD), (TOK, KV * HEAD)
    vmem = pl.BlockSpec(memory_space=pltpu.VMEM)
    dma = pltpu.SemaphoreType.DMA
    outs = pl.pallas_call(
        kernel,
        out_shape=(
            jax.ShapeDtypeStruct(wide, jnp.bfloat16),
            jax.ShapeDtypeStruct(wide, jnp.bfloat16),
            jax.ShapeDtypeStruct(narrow, jnp.bfloat16),
            jax.ShapeDtypeStruct(narrow, jnp.bfloat16),
            jax.ShapeDtypeStruct((16, HEAD), jnp.float32),
        ),
        in_specs=[vmem] * 7,
        out_specs=(vmem,) * 5,
        scratch_shapes=[
            pltpu.VMEM((KV, BLOCKS, 2 * TOK, HEAD), jnp.bfloat16),
            pltpu.VMEM((BLOCKS, 16, TOK), jnp.bfloat16),
            pltpu.VMEM((BLOCKS, TOK, TOK), jnp.float32),
            pltpu.VMEM((KV, WIDTH, HEAD), jnp.bfloat16),
            pltpu.VMEM((KV, WIDTH, HEAD), jnp.bfloat16),
            pltpu.VMEM((KV, HEAD, WIDTH), jnp.bfloat16),
            pltpu.VMEM((KV, BLOCKS, TOK, HEAD), jnp.bfloat16),
            pltpu.VMEM((KV, BLOCKS, TOK, HEAD), jnp.float32),
            pltpu.VMEM((KV, BLOCKS, TOK, WIDTH), jnp.float32),
            pltpu.VMEM((KV, 8, WIDTH), jnp.float32),
            pltpu.VMEM((BLOCKS, TOK, WIDTH), jnp.bfloat16),
            pltpu.VMEM((BLOCKS, TOK, WIDTH), jnp.bfloat16),
            pltpu.VMEM((KV, BLOCKS, 2 * TOK, HEAD), jnp.float32),
            pltpu.VMEM((KV, SPAN, 2 * TOK, HEAD), jnp.bfloat16),
            pltpu.VMEM((KV, SPAN, 2 * TOK, HEAD), jnp.bfloat16),
            dma((KV, SPAN)),
            dma((KV, SPAN)),
            dma((SPAN,)),
            dma((SPAN,)),
            dma((KV, SPAN)),
            dma((KV, SPAN)),
        ],
        compiler_params=pltpu.CompilerParams(
            collective_id=0, has_side_effects=True, vmem_limit_bytes=48 << 20
        ),
        cost_estimate=pl.CostEstimate(
            flops=2 * 6 * TOK * BLOCKS * TOK * HEAD * KV * GROUP,
            bytes_accessed=3 << 20,
            transcendentals=TOK * BLOCKS * TOK * KV * GROUP,
        ),
        name="attention",
    )(
        query_raw[0],
        key_raw[0],
        values[0],
        query_gain[None],
        key_gain[None],
        segment_ids,
        grad_attended[0],
    )
    attended, grad_query, grad_key, grad_values, gains = outs
    gains = lax.psum(jnp.sum(gains.reshape(2, 8, HEAD), axis=1), ("dp", "seq"))
    return (
        attended[None],
        grad_query[None],
        grad_key[None],
        grad_values[None],
        gains[0],
        gains[1],
    )


def solution(mesh):
    row = P("dp", "seq", None)
    return jax.shard_map(
        local,
        mesh=mesh,
        in_specs=(row, row, row, P(), P(), P("dp", "seq"), row),
        out_specs=(row, row, row, row, P(), P()),
        check_vma=False,
    )
```

time: 568 us -> 233 us (0.41)
  waiting for transfers between devices: 203 us -> 0 us
  starting transfers between devices: 150 us -> 0 us
  Pallas kernels: 0 us -> 114 us
  matrix products: 38.1 us -> 0 us
  local copies, waits for them, and re-layouts: 30.9 us -> 8.14 us
  other arithmetic: 20.2 us -> 0.02 us
  blocking collectives: 119 us -> 108 us
    ppermute x28 -> x0, waiting for transfers between devices: 203 us -> none  [shifted(): lax.ppermute(value, axis, [(source, source + steps) for source in range(i...]
    ppermute x28 -> x0, starting transfers between devices: 150 us -> none  [shifted(): lax.ppermute(value, axis, [(source, source + steps) for source in range(i...]
    pallas_call x0 -> x1, Pallas kernels: none -> 114 us  [local(): pl.pallas_call(kernel, out_shape=(jax.ShapeDtypeStruct(wide, jnp.bfloat16...]
    dot_general x28 -> x0, matrix products: 38.1 us -> none  [the longest x4 8.58 us: group_backward(): jnp.einsum('tgh,wh->tgw', grad_out, value_rows, preferred_element_type=jn...]
    unnamed x64 -> x18, local copies, waits for them, and re-layouts: 21.1 us -> 7.63 us
    psum x1, blocking collectives: 119 us -> 108 us  [local(): gains = lax.psum(jnp.sum(gains.reshape(2, 8, HEAD), axis=1), ('dp', 'seq'))]
    reduce_sum x11 -> x1, other arithmetic: 7.15 us -> 0.02 us  [local(): gains = lax.psum(jnp.sum(gains.reshape(2, 8, HEAD), axis=1), ('dp', 'seq'))]
  transfers between devices with their start and end apart: 28 -> 0, of which waited for: 16 -> 0; matrix products, arithmetic and copies ran while one was open for 4% -> 0% of each run, Pallas kernels for 0% -> 0%
where the time goes in v1:
time: 233 us; the launch traced here: 231 us
  Pallas kernels  114 us (49%)
  blocking collectives  108 us (46%)
  local copies, waits for them, and re-layouts  8.14 us (3%)
    pallas_call x1, Pallas kernels, local(): pl.pallas_call(kernel, out_shape=(jax.ShapeDtypeStruct(wide, jnp.bfloat16...  114 us
    psum x1, blocking collectives, local(): gains = lax.psum(jnp.sum(gains.reshape(2, 8, HEAD), axis=1), ('dp', 'seq'))  108 us
    unnamed x18, local copies, waits for them, and re-layouts  7.63 us

profile of v1, /device:TPU:24, one launch (start us, length us, event | category | flops | bytes accessed | tf_op | source)
XLA Modules:
  0.0 231.0 jit_solution(4001256841511376213)
XLA Ops:
  0.6 0.0 copy-start.4
  0.6 0.0 copy-start.5
  0.7 0.0 copy-start.6
  0.7 0.6 copy-done.4
  1.3 0.0 copy-done.5
  1.3 0.0 copy-done.6
  1.3 0.0 copy-start
  1.3 1.1 copy-done
  2.4 0.0 copy-start.1
  2.4 1.1 copy-done.1
  3.5 0.0 copy-start.2
  3.5 0.9 copy-done.2
  4.4 0.0 copy-start.3
  4.4 0.9 copy-done.3
  5.3 113.9 %attention.1 = (bf16[128,2560]{1,0:T(8,128)(2,1)S(1)}, bf16[128,2560]{1,0:T(8,128)(2,1)S(1)}, bf16[128,512]{1,0:T(8,128)(2,1)S(1)}, bf16[128,512]{1,0:T(8,128)(2,1)S(1)}, f32[16,128]{1,0:T(8,128)S(1)}) custom-call(bf16[128,2560]{1,0:T(8,128)(2,1)S(1)} %bitcast.20, bf16[128,512]{1,0:T(8,128)(2,1)S(1)} %bitcast.22, bf16[128,512]{1,0:T(8,128)(2,1)S(1)} %bitcast.23, ...), custom_call_target="tpu_custom_call" | custom-call | flops 4026531840 | bytes 3145728 | tf_op jit(solution)/shard_map/attention/pallas_call | solution.py:283
  119.2 108.3 %psum.7 = f32[2,128]{1,0:T(2,128)S(1)} all-reduce(f32[2,128]{1,0:T(2,128)S(1)} %bitcast_reduce_fusion), channel_id=1, replica_groups=mesh['dp'=8,'seq'=64] {'dp','seq'}, use_global_device_ids=true, to_apply=%region_1.0 | all-reduce | flops 256 | bytes 2048 | tf_op jit(solution)/shard_map/psum | solution.py:336
  227.5 0.5 slice_bitcast_fusion
  228.0 0.8 copy.17
  228.8 0.8 copy.18
  229.7 0.7 copy.19
  230.3 0.7 copy.20
  (1 shorter events, 0.0 us)
Async XLA Ops:
  0.6 0.7 copy-start.4
  0.6 0.7 copy-start.5
  0.7 0.7 copy-start.6
  1.3 1.1 copy-start
  2.4 1.1 copy-start.1
  3.5 0.9 copy-start.2
  4.4 0.9 copy-start.3

commit v2 on v1

v2 whole, which is shorter than its diff:
```python
import math

import jax
import jax.numpy as jnp
from jax import lax
from jax.experimental import pallas as pl
from jax.experimental.pallas import tpu as pltpu
from jax.sharding import PartitionSpec as P

SPAN = 7
BLOCKS = SPAN + 1
HEAD = 128
TOK = 128
KV = 4
GROUP = 5
OFFSETS = (0, 1, 6, 7)
ROW = 16
WIDTH = GROUP * TOK
ROUNDS = OFFSETS[-1] + 2 * SPAN + 1
TAIL = OFFSETS[-1] + SPAN
SWAPS = (0, 1, 2, 4, 6, 8)
EPSILON = 1e-06
LIMIT = 60
SCALE = HEAD**-0.5
MESH = pl.DeviceIdType.MESH

NT = (((1,), (1,)), ((), ()))
NN = (((1,), (0,)), ((), ()))
TN = (((0,), (0,)), ((), ()))


def dot(a, b, dims):
    return lax.dot_general(a, b, dims, preferred_element_type=jnp.float32)


def normalize(rows):
    inverse = lax.rsqrt(jnp.mean(rows * rows, axis=-1, keepdims=True) + EPSILON)
    return rows * inverse, inverse


def norm_backward(grad, unit, inverse, gain):
    scaled = grad * gain
    return inverse * (scaled - unit * jnp.mean(scaled * unit, axis=-1, keepdims=True))


def lanes(head):
    return pl.ds(pl.multiple_of(head * HEAD, HEAD), HEAD)


def kernel(
    query_hbm, key_hbm, value_hbm, query_gain_ref, key_gain_ref, segment_ref, grad_hbm,
    attended_hbm, grad_query_hbm, grad_key_hbm, grad_value_hbm, gains_ref,
    window, ids, bias, query_norm, grad_rows, grad_cols, key_norm, key_unit, scores, row_max,
    weights, grad_scores, partial, outgoing, incoming,
    query_ref, grad_ref, attended_ref, grad_query_ref, grad_key_ref, grad_value_ref, sums, exchange,
    up_send, up_recv, id_send, id_recv, down_send, down_recv, swap_send, swap_recv, load, wide_store, narrow_store,
):
    count = lax.axis_size("seq")
    me = lax.axis_index("seq")
    dp = lax.axis_index("dp")
    after = lax.rem(me + 1, count)
    before = lax.rem(me + count - 1, count)

    place = lax.rem(me, ROW)
    sizes = (lax.axis_size("dp"), count // ROW, 4, 4)
    mine = (dp, me // ROW, lax.rem(place, 4), place // 4)

    def peer(phase, at):
        if phase == 0:
            return at, me
        return dp, me + (at - mine[phase]) * (0, ROW, 1, 4)[phase]

    loads = []
    for head in range(KV):
        at = slice(head * HEAD, (head + 1) * HEAD)
        loads.append((key_hbm.at[:, at], window.at[head, 0, pl.ds(0, TOK)]))
        loads.append((value_hbm.at[:, at], window.at[head, 0, pl.ds(TOK, TOK)]))
    loads.append((query_hbm, query_ref))
    loads.append((grad_hbm, grad_ref))
    loads = [pltpu.make_async_copy(a, b, load.at[i]) for i, (a, b) in enumerate(loads)]
    for copy in loads:
        copy.start()

    barrier = pltpu.get_barrier_semaphore()
    greeted = 2
    for neighbour in (after, before):
        pl.semaphore_signal(barrier, inc=1, device_id=(dp, neighbour), device_id_type=MESH)
    for phase in range(4):
        for j in range(1, sizes[phase]):
            if phase == 3 and j == 2:
                continue
            target = peer(phase, lax.rem(mine[phase] + j, sizes[phase]))
            pl.semaphore_signal(barrier, inc=1, device_id=target, device_id_type=MESH)
            greeted += 1

    def swap(phase, j, slot):
        return pltpu.make_async_remote_copy(
            src_ref=exchange.at[phase, slot],
            dst_ref=exchange.at[phase, slot],
            send_sem=swap_send.at[phase, j],
            recv_sem=swap_recv.at[phase, slot],
            device_id=peer(phase, lax.rem(mine[phase] + j, sizes[phase])),
            device_id_type=MESH,
        )

    def swap_start(phase):
        if phase == 4:
            slot = lax.rem(mine[3] + 3, 4)
            swap(3, 1, slot).start()
            return
        exchange[phase, mine[phase]] = sums[...]
        for j in range(1, sizes[phase]):
            if phase < 3 or j != 2:
                swap(phase, j, mine[phase]).start()

    def swap_finish(phase):
        if phase == 4:
            swap(3, 1, lax.rem(mine[3] + 2, 4)).wait_recv()
            swap(3, 1, lax.rem(mine[3] + 3, 4)).wait_send()
            phase = 3
        else:
            for j in range(1, sizes[phase]):
                if phase < 3 or j != 2:
                    swap(phase, j, lax.rem(mine[phase] + j, sizes[phase])).wait_recv()
                    swap(phase, j, mine[phase]).wait_send()
            if phase == 3:
                return
        total = exchange[phase, 0]
        for slot in range(1, sizes[phase]):
            total = total + exchange[phase, slot]
        sums[...] = total

    def up(head, step, part):
        rows = pl.ds(part * TOK, TOK)
        return pltpu.make_async_remote_copy(
            src_ref=window.at[head, step, rows],
            dst_ref=window.at[head, step + 1, rows],
            send_sem=up_send.at[head, step, part],
            recv_sem=up_recv.at[head, step, part],
            device_id=(dp, after),
            device_id_type=MESH,
        )

    def up_ids(step):
        return pltpu.make_async_remote_copy(
            src_ref=ids.at[step],
            dst_ref=ids.at[step + 1],
            send_sem=id_send.at[step],
            recv_sem=id_recv.at[step],
            device_id=(dp, after),
            device_id_type=MESH,
        )

    def down(head, step, part):
        rows = pl.ds(part * TOK, TOK)
        return pltpu.make_async_remote_copy(
            src_ref=outgoing.at[head, step, rows],
            dst_ref=incoming.at[head, step, rows],
            send_sem=down_send.at[head, step, part],
            recv_sem=down_recv.at[head, step, part],
            device_id=(dp, before),
            device_id_type=MESH,
        )

    own_ids = segment_ref[...].astype(jnp.float32)
    ids[0] = jnp.broadcast_to(own_ids, (16, TOK)).astype(jnp.bfloat16)
    def prepare(head):
        group, member = head // GROUP, lax.rem(head, GROUP)
        rows = pl.ds(pl.multiple_of(member * TOK, TOK), TOK)
        unit, _ = normalize(query_ref[:, lanes(head)].astype(jnp.float32))
        query_norm[group, rows, :] = (unit * query_gain_ref[...]).astype(jnp.bfloat16)
        grad = grad_ref[:, lanes(head)]
        grad_rows[group, rows, :] = grad
        grad_cols[group, :, rows] = grad.astype(jnp.float32).T.astype(jnp.bfloat16)

    def mask_block(step):
        key_ids = jnp.broadcast_to(ids[step, 0:16, :].astype(jnp.float32)[0:1], (TOK, TOK)).T
        seen = key_ids == own_ids
        key_at = lax.broadcasted_iota(jnp.int32, (TOK, TOK), 0)
        query_at = lax.broadcasted_iota(jnp.int32, (TOK, TOK), 1)
        seen = seen & (key_at <= query_at + jnp.where(step > 0, TOK, 0))
        bias[step] = jnp.where(seen, 0.0, -1e30)

    def score_block(head, step):
        unit, _ = normalize(window[head, step, :TOK].astype(jnp.float32))
        key_unit[head, step] = unit
        keys = (unit * key_gain_ref[...]).astype(jnp.bfloat16)
        key_norm[head, step] = keys
        raw = dot(keys, query_norm[head], NT) * (SCALE * math.log2(math.e))
        block_bias = bias[step]
        for member in range(GROUP):
            at = slice(member * TOK, (member + 1) * TOK)
            part = raw[:, at] + block_bias
            scores[head, step, :, at] = part
            top = jnp.max(part.reshape(TOK // 8, 8, TOK), axis=0)
            row_max[head, :, at] = jnp.maximum(row_max[head, :, at], top)

    def head_work(head):
        top = jnp.max(row_max[head], axis=0, keepdims=True)

        def exponent(step, total):
            part = jnp.exp2(scores[head, step] - top)
            scores[head, step] = part
            return total + jnp.sum(part.reshape(TOK // 8, 8, WIDTH), axis=0)

        total = lax.fori_loop(0, BLOCKS, exponent, jnp.zeros((8, WIDTH), jnp.float32))
        inverse = 1.0 / jnp.sum(total, axis=0, keepdims=True)
        rows = BLOCKS * TOK
        weights[...] = (scores[head].reshape(rows, WIDTH) * inverse).astype(jnp.bfloat16)
        partial[head, :, TOK:] = dot(weights[...], grad_rows[head], NN).reshape(BLOCKS, TOK, HEAD)
        outgoing[head, 0, TOK:] = partial[head, SPAN, TOK:].astype(jnp.bfloat16)
        down(head, 0, 1).start()
        value_rows = window[head, :, TOK:].reshape(rows, HEAD)
        output = dot(value_rows, weights[...], TN)
        output = output.astype(jnp.bfloat16).astype(jnp.float32)
        correction = jnp.sum(output * grad_cols[head].astype(jnp.float32), axis=0, keepdims=True)
        grad_prob = dot(value_rows, grad_rows[head], NT)
        grad_scores[...] = (
            scores[head].reshape(rows, WIDTH) * (inverse * SCALE) * (grad_prob - correction)
        ).astype(jnp.bfloat16)
        grad_key = dot(grad_scores[...], query_norm[head], NN)
        partial[head, :, :TOK] = grad_key.reshape(BLOCKS, TOK, HEAD)
        outgoing[head, 0, :TOK] = partial[head, SPAN, :TOK].astype(jnp.bfloat16)
        down(head, 0, 0).start()

        for member in range(GROUP):
            at = slice(member * TOK, (member + 1) * TOK)
            attended_ref[:, lanes(head * GROUP + member)] = output[:, at].T.astype(jnp.bfloat16)
        sums[8:] += jnp.sum((grad_key * key_unit[head].reshape(rows, HEAD)).reshape(-1, 8, HEAD), axis=0)
        grad_query = dot(key_norm[head].reshape(rows, HEAD), grad_scores[...], TN)
        for member in range(GROUP):
            at = slice(member * TOK, (member + 1) * TOK)
            where = lanes(head * GROUP + member)
            unit, query_inverse = normalize(query_ref[:, where].astype(jnp.float32))
            grad = grad_query[:, at].T
            sums[:8] += jnp.sum((grad * unit).reshape(TOK // 8, 8, HEAD), axis=0)
            grad_query_ref[:, where] = norm_backward(
                grad, unit, query_inverse, query_gain_ref[...]
            ).astype(jnp.bfloat16)

    def narrow(head, part):
        at = pl.ds(head * HEAD, HEAD)
        source = (grad_key_ref, grad_value_ref)[part]
        target = (grad_key_hbm, grad_value_hbm)[part]
        return pltpu.make_async_copy(
            source.at[:, at], target.at[:, at], narrow_store.at[head, part]
        )

    def wide(head, part):
        at = pl.ds(pl.multiple_of(head * GROUP * HEAD, HEAD), GROUP * HEAD)
        source = (attended_ref, grad_query_ref)[part]
        target = (attended_hbm, grad_query_hbm)[part]
        return pltpu.make_async_copy(
            source.at[:, at], target.at[:, at], wide_store.at[head, part]
        )

    def receive_up(head, step):
        @pl.when((step >= 0) & (step <= SPAN))
        def _():
            if head == 0:

                @pl.when(step > 0)
                def _():
                    up_ids(step - 1).wait_recv()

                @pl.when(step < SPAN)
                def _():
                    up_ids(step).start()

            for part in range(2):

                @pl.when(step > 0)
                def _():
                    up(head, step - 1, part).wait_recv()

                @pl.when(step < SPAN)
                def _():
                    up(head, step, part).start()

    def receive_down(head, back):
        @pl.when((back >= 1) & (back < SPAN))
        def _():
            for part in (1, 0):
                rows = slice(part * TOK, (part + 1) * TOK)
                down(head, back - 1, part).wait_recv()
                total = incoming[head, back - 1, rows].astype(jnp.float32)
                total = total + partial[head, SPAN - back, rows]
                outgoing[head, back, rows] = total.astype(jnp.bfloat16)
                down(head, back, part).start()

        @pl.when(back == SPAN)
        def _():
            at = slice(head * HEAD, (head + 1) * HEAD)
            down(head, SPAN - 1, 1).wait_recv()
            total = incoming[head, SPAN - 1, TOK:].astype(jnp.float32) + partial[head, 0, TOK:]
            grad_value_ref[:, at] = total.astype(jnp.bfloat16)
            narrow(head, 1).start()
            down(head, SPAN - 1, 0).wait_recv()
            total = incoming[head, SPAN - 1, :TOK].astype(jnp.float32) + partial[head, 0, :TOK]
            unit, inverse = normalize(window[head, 0, :TOK].astype(jnp.float32))
            grad_key_ref[:, at] = norm_backward(
                total, unit, inverse, key_gain_ref[...]
            ).astype(jnp.bfloat16)
            narrow(head, 0).start()

    def work(head, step):
        @pl.when((step >= 1) & (step <= SPAN))
        def _():
            @pl.when(head == 0)
            def _():
                mask_block(step)

            score_block(head, step)

        @pl.when(step == SPAN)
        def _():
            head_work(head)
            wide(head, 0).start()
            wide(head, 1).start()

    row_max[...] = jnp.full(row_max.shape, -jnp.inf, jnp.float32)
    sums[...] = jnp.zeros(sums.shape, jnp.float32)
    for copy in loads:
        copy.wait()

    def prepare_one(head, carry):
        prepare(head)
        return carry

    def own_one(head, carry):
        score_block(head, 0)
        return carry

    lax.fori_loop(0, KV * GROUP, prepare_one, 0)
    mask_block(0)
    lax.fori_loop(0, KV, own_one, 0)
    pl.semaphore_wait(barrier, greeted)

    def offset(head):
        return sum(
            jnp.where(head >= k, OFFSETS[k] - OFFSETS[k - 1], 0) for k in range(1, KV)
        )

    def one_round(index, carry):
        for head in range(KV):
            receive_up(head, index - OFFSETS[head])

        def second(head, inner):
            work(head, index - offset(head))
            return inner

        lax.fori_loop(0, KV, second, 0)
        for head in range(KV):
            receive_down(head, index - OFFSETS[head] - SPAN)

        for phase in range(5):

            @pl.when(index == TAIL + SWAPS[phase])
            def _():
                if phase > 0:
                    swap_finish(phase - 1)
                swap_start(phase)

        return carry

    lax.fori_loop(0, ROUNDS, one_round, 0)

    def drain(head, carry):
        def one(step, inner):
            for part in range(2):
                up(head, step, part).wait_send()
                down(head, step, part).wait_send()

            @pl.when(head == 0)
            def _():
                up_ids(step).wait_send()

            return inner

        return lax.fori_loop(0, SPAN, one, carry)

    lax.fori_loop(0, KV, drain, 0)
    for head in range(KV):
        for part in range(2):
            wide(head, part).wait()
            narrow(head, part).wait()
    swap_finish(4)
    gains_ref[...] = jnp.sum(sums[...].reshape(2, 8, HEAD), axis=1)


def deliver(*refs):
    sources, gains, targets = refs[:4], refs[4], refs[5:9]
    query_gain, key_gain = refs[9:11]
    held, loaded, stored = refs[11:15], refs[15], refs[16]
    loads, stores = [], []
    for i in range(4):
        loads.append(pltpu.make_async_copy(sources[i], held[i], loaded.at[i]))
        stores.append(pltpu.make_async_copy(held[i], targets[i], stored.at[i]))
    for copy in loads:
        copy.start()
    query_gain[...] = gains[0:1]
    key_gain[...] = gains[1:2]
    for load, store in zip(loads, stores):
        load.wait()
        store.start()
    for copy in stores:
        copy.wait()


def local(query_raw, key_raw, values, query_gain, key_gain, segment_ids, grad_attended):
    wide, narrow = (TOK, KV * GROUP * HEAD), (TOK, KV * HEAD)
    vmem = pl.BlockSpec(memory_space=pltpu.VMEM)
    hbm = pl.BlockSpec(memory_space=pltpu.HBM)
    dma = pltpu.SemaphoreType.DMA
    outs_like = (
        jax.ShapeDtypeStruct(wide, jnp.bfloat16),
        jax.ShapeDtypeStruct(wide, jnp.bfloat16),
        jax.ShapeDtypeStruct(narrow, jnp.bfloat16),
        jax.ShapeDtypeStruct(narrow, jnp.bfloat16),
        jax.ShapeDtypeStruct((2, HEAD), jnp.float32),
    )
    outs = pl.pallas_call(
        kernel,
        out_shape=outs_like,
        in_specs=[hbm, hbm, hbm, vmem, vmem, vmem, hbm],
        out_specs=(hbm,) * 4 + (vmem,),
        scratch_shapes=[
            pltpu.VMEM((KV, BLOCKS, 2 * TOK, HEAD), jnp.bfloat16),
            pltpu.VMEM((BLOCKS, 16, TOK), jnp.bfloat16),
            pltpu.VMEM((BLOCKS, TOK, TOK), jnp.float32),
            pltpu.VMEM((KV, WIDTH, HEAD), jnp.bfloat16),
            pltpu.VMEM((KV, WIDTH, HEAD), jnp.bfloat16),
            pltpu.VMEM((KV, HEAD, WIDTH), jnp.bfloat16),
            pltpu.VMEM((KV, BLOCKS, TOK, HEAD), jnp.bfloat16),
            pltpu.VMEM((KV, BLOCKS, TOK, HEAD), jnp.float32),
            pltpu.VMEM((KV, BLOCKS, TOK, WIDTH), jnp.float32),
            pltpu.VMEM((KV, 8, WIDTH), jnp.float32),
            pltpu.VMEM((BLOCKS * TOK, WIDTH), jnp.bfloat16),
            pltpu.VMEM((BLOCKS * TOK, WIDTH), jnp.bfloat16),
            pltpu.VMEM((KV, BLOCKS, 2 * TOK, HEAD), jnp.float32),
            pltpu.VMEM((KV, SPAN, 2 * TOK, HEAD), jnp.bfloat16),
            pltpu.VMEM((KV, SPAN, 2 * TOK, HEAD), jnp.bfloat16),
            pltpu.VMEM(wide, jnp.bfloat16),
            pltpu.VMEM(wide, jnp.bfloat16),
            pltpu.VMEM(wide, jnp.bfloat16),
            pltpu.VMEM(wide, jnp.bfloat16),
            pltpu.VMEM(narrow, jnp.bfloat16),
            pltpu.VMEM(narrow, jnp.bfloat16),
            pltpu.VMEM((16, HEAD), jnp.float32),
            pltpu.VMEM((4, 8, 16, HEAD), jnp.float32),
            dma((KV, SPAN, 2)),
            dma((KV, SPAN, 2)),
            dma((SPAN,)),
            dma((SPAN,)),
            dma((KV, SPAN, 2)),
            dma((KV, SPAN, 2)),
            dma((4, 8)),
            dma((4, 8)),
            dma((2 * KV + 2,)),
            dma((KV, 2)),
            dma((KV, 2)),
        ],
        compiler_params=pltpu.CompilerParams(
            collective_id=0, has_side_effects=True, vmem_limit_bytes=LIMIT << 20
        ),
        cost_estimate=pl.CostEstimate(
            flops=2 * 6 * TOK * BLOCKS * TOK * HEAD * KV * GROUP,
            bytes_accessed=3 << 20,
            transcendentals=TOK * BLOCKS * TOK * KV * GROUP,
        ),
        name="attention",
    )(
        query_raw[0],
        key_raw[0],
        values[0],
        query_gain[None],
        key_gain[None],
        segment_ids,
        grad_attended[0],
    )
    attended, grad_query, grad_key, grad_values, grad_query_gain, grad_key_gain = pl.pallas_call(
        deliver,
        out_shape=outs_like[:4] + (jax.ShapeDtypeStruct((1, HEAD), jnp.float32),) * 2,
        in_specs=[hbm] * 4 + [vmem],
        out_specs=(hbm,) * 4 + (vmem,) * 2,
        scratch_shapes=[
            pltpu.VMEM(wide, jnp.bfloat16),
            pltpu.VMEM(wide, jnp.bfloat16),
            pltpu.VMEM(narrow, jnp.bfloat16),
            pltpu.VMEM(narrow, jnp.bfloat16),
            dma((4,)),
            dma((4,)),
        ],
        name="deliver",
    )(*outs)
    return (
        attended[None],
        grad_query[None],
        grad_key[None],
        grad_values[None],
        grad_query_gain[0],
        grad_key_gain[0],
    )


def solution(mesh):
    row = P("dp", "seq", None)
    return jax.shard_map(
        local,
        mesh=mesh,
        in_specs=(row, row, row, P(), P(), P("dp", "seq"), row),
        out_specs=(row, row, row, row, P(), P()),
        check_vma=False,
    )
```

time: 233 us -> 115 us (0.49)
  blocking collectives: 108 us -> 0 us
  local copies, waits for them, and re-layouts: 8.14 us -> 0 us
    psum x1 -> x0, blocking collectives: 108 us -> none  [local(): gains = lax.psum(jnp.sum(gains.reshape(2, 8, HEAD), axis=1), ('dp', 'seq'))]
    unnamed x18 -> x0, local copies, waits for them, and re-layouts: 7.63 us -> none
    pallas_call x1 -> x2, Pallas kernels: 114 us -> 114 us  [the longest x1 110 us: local(): pl.pallas_call(kernel, out_shape=outs_like, in_specs=[hbm, hbm, hbm, vmem...]
where the time goes in v2:
time: 115 us; the launch traced here: 114 us
  Pallas kernels  114 us (99%)
    pallas_call x1, Pallas kernels, local(): pl.pallas_call(kernel, out_shape=outs_like, in_specs=[hbm, hbm, hbm, vmem...  110 us
    pallas_call x1, Pallas kernels, local(): pl.pallas_call(deliver, out_shape=outs_like[:4] + (jax.ShapeDtypeStruct((...  3.45 us

profile of v2, /device:TPU:24, one launch (start us, length us, event | category | flops | bytes accessed | tf_op | source)
XLA Modules:
  0.0 114.3 jit_solution(9564893488965642761)
XLA Ops:
  0.6 110.2 %attention.1 = (bf16[128,2560]{1,0:T(8,128)(2,1)}, bf16[128,2560]{1,0:T(8,128)(2,1)}, bf16[128,512]{1,0:T(8,128)(2,1)}, bf16[128,512]{1,0:T(8,128)(2,1)}, f32[2,128]{1,0:T(2,128)}) custom-call(bf16[128,2560]{1,0:T(8,128)(2,1)} %bitcast.12, bf16[128,512]{1,0:T(8,128)(2,1)} %bitcast.16, bf16[128,512]{1,0:T(8,128)(2,1)} %bitcast.17, f32[1,128]{1,0:T(1,128)} %bitcast.20, ...), custom_call_target="tpu_custom_call" | custom-call | flops 4026531840 | bytes 3145728 | tf_op jit(solution)/shard_map/attention/pallas_call | solution.py:422
  110.9 3.5 %deliver.1 = (bf16[128,2560]{1,0:T(8,128)(2,1)}, bf16[128,2560]{1,0:T(8,128)(2,1)}, bf16[128,512]{1,0:T(8,128)(2,1)}, bf16[128,512]{1,0:T(8,128)(2,1)}, f32[1,128]{1,0:T(1,128)}, /*index=5*/f32[1,128]{1,0:T(1,128)}) custom-call(bf16[128,2560]{1,0:T(8,128)(2,1)} %get-tuple-element.17.refs_0_, bf16[128,2560]{1,0:T(8,128)(2,1)} %get-tuple-element.18.refs_1_, ...), custom_call_target="tpu_custom_call" | custom-call | tf_op jit(solution)/shard_map/deliver/pallas_call | solution.py:481

commit v3 on v2

--- a/solution.py
+++ b/solution.py
@@ -13,14 +13,15 @@
 TOK = 128
 KV = 4
 GROUP = 5
-OFFSETS = (0, 1, 6, 7)
+OFFSETS = (0, 0, 7, 7)
 ROW = 16
 WIDTH = GROUP * TOK
 ROUNDS = OFFSETS[-1] + 2 * SPAN + 1
 TAIL = OFFSETS[-1] + SPAN
-SWAPS = (0, 1, 2, 4, 6, 8)
+SWAPS = (0, 1, 2, 3, 5, 6)
 EPSILON = 1e-06
 LIMIT = 60
+PIECES = 4
 SCALE = HEAD**-0.5
 MESH = pl.DeviceIdType.MESH
 
@@ -205,28 +206,43 @@
 
         total = lax.fori_loop(0, BLOCKS, exponent, jnp.zeros((8, WIDTH), jnp.float32))
         inverse = 1.0 / jnp.sum(total, axis=0, keepdims=True)
-        rows = BLOCKS * TOK
-        weights[...] = (scores[head].reshape(rows, WIDTH) * inverse).astype(jnp.bfloat16)
-        partial[head, :, TOK:] = dot(weights[...], grad_rows[head], NN).reshape(BLOCKS, TOK, HEAD)
-        outgoing[head, 0, TOK:] = partial[head, SPAN, TOK:].astype(jnp.bfloat16)
+        near, rows = SPAN * TOK, BLOCKS * TOK
+
+        weights[near:] = (scores[head, SPAN] * inverse).astype(jnp.bfloat16)
+        grad_value = dot(weights[near:], grad_rows[head], NN)
+        outgoing[head, 0, TOK:] = grad_value.astype(jnp.bfloat16)
         down(head, 0, 1).start()
-        value_rows = window[head, :, TOK:].reshape(rows, HEAD)
-        output = dot(value_rows, weights[...], TN)
+
+        weights[:near] = (scores[head, :SPAN].reshape(near, WIDTH) * inverse).astype(jnp.bfloat16)
+        output = dot(window[head, :, TOK:].reshape(rows, HEAD), weights[...], TN)
         output = output.astype(jnp.bfloat16).astype(jnp.float32)
         correction = jnp.sum(output * grad_cols[head].astype(jnp.float32), axis=0, keepdims=True)
+        scaled = inverse * SCALE
+
+        grad_prob = dot(window[head, SPAN, TOK:], grad_rows[head], NT)
+        grad_scores[near:] = (
+            scores[head, SPAN] * scaled * (grad_prob - correction)
+        ).astype(jnp.bfloat16)
+        grad_key = dot(grad_scores[near:], query_norm[head], NN)
+        outgoing[head, 0, :TOK] = grad_key.astype(jnp.bfloat16)
+        down(head, 0, 0).start()
+        sums[8:] += jnp.sum((grad_key * key_unit[head, SPAN]).reshape(-1, 8, HEAD), axis=0)
+
+        grad_value = dot(weights[:near], grad_rows[head], NN)
+        partial[head, :, TOK:] = grad_value.reshape(SPAN, TOK, HEAD)
+        value_rows = window[head, :SPAN, TOK:].reshape(near, HEAD)
         grad_prob = dot(value_rows, grad_rows[head], NT)
-        grad_scores[...] = (
-            scores[head].reshape(rows, WIDTH) * (inverse * SCALE) * (grad_prob - correction)
+        grad_scores[:near] = (
+            scores[head, :SPAN].reshape(near, WIDTH) * scaled * (grad_prob - correction)
         ).astype(jnp.bfloat16)
-        grad_key = dot(grad_scores[...], query_norm[head], NN)
-        partial[head, :, :TOK] = grad_key.reshape(BLOCKS, TOK, HEAD)
-        outgoing[head, 0, :TOK] = partial[head, SPAN, :TOK].astype(jnp.bfloat16)
-        down(head, 0, 0).start()
+        grad_key = dot(grad_scores[:near], query_norm[head], NN)
+        partial[head, :, :TOK] = grad_key.reshape(SPAN, TOK, HEAD)
+        units = key_unit[head, :SPAN].reshape(near, HEAD)
+        sums[8:] += jnp.sum((grad_key * units).reshape(-1, 8, HEAD), axis=0)
 
         for member in range(GROUP):
             at = slice(member * TOK, (member + 1) * TOK)
             attended_ref[:, lanes(head * GROUP + member)] = output[:, at].T.astype(jnp.bfloat16)
-        sums[8:] += jnp.sum((grad_key * key_unit[head].reshape(rows, HEAD)).reshape(-1, 8, HEAD), axis=0)
         grad_query = dot(key_norm[head].reshape(rows, HEAD), grad_scores[...], TN)
         for member in range(GROUP):
             at = slice(member * TOK, (member + 1) * TOK)
@@ -320,21 +336,23 @@
 
     row_max[...] = jnp.full(row_max.shape, -jnp.inf, jnp.float32)
     sums[...] = jnp.zeros(sums.shape, jnp.float32)
-    for copy in loads:
+    for copy in loads[:-2]:
         copy.wait()
-
-    def prepare_one(head, carry):
-        prepare(head)
-        return carry
-
-    def own_one(head, carry):
+    pl.semaphore_wait(barrier, greeted)
+
+    def ready(head):
+        def one(member, carry):
+            prepare(head * GROUP + member)
+            return carry
+
+        @pl.when(head == 0)
+        def _():
+            for copy in loads[-2:]:
+                copy.wait()
+            mask_block(0)
+
+        lax.fori_loop(0, GROUP, one, 0)
         score_block(head, 0)
-        return carry
-
-    lax.fori_loop(0, KV * GROUP, prepare_one, 0)
-    mask_block(0)
-    lax.fori_loop(0, KV, own_one, 0)
-    pl.semaphore_wait(barrier, greeted)
 
     def offset(head):
         return sum(
@@ -349,17 +367,22 @@
             work(head, index - offset(head))
             return inner
 
+        @pl.when(index < KV)
+        def _():
+            ready(index)
+
         lax.fori_loop(0, KV, second, 0)
         for head in range(KV):
             receive_down(head, index - OFFSETS[head] - SPAN)
 
-        for phase in range(5):
+        for phase in range(6):
 
             @pl.when(index == TAIL + SWAPS[phase])
             def _():
                 if phase > 0:
                     swap_finish(phase - 1)
-                swap_start(phase)
+                if phase < 5:
+                    swap_start(phase)
 
         return carry
 
@@ -384,7 +407,6 @@
         for part in range(2):
             wide(head, part).wait()
             narrow(head, part).wait()
-    swap_finish(4)
     gains_ref[...] = jnp.sum(sums[...].reshape(2, 8, HEAD), axis=1)
 
 
@@ -394,8 +416,14 @@
     held, loaded, stored = refs[11:15], refs[15], refs[16]
     loads, stores = [], []
     for i in range(4):
-        loads.append(pltpu.make_async_copy(sources[i], held[i], loaded.at[i]))
-        stores.append(pltpu.make_async_copy(held[i], targets[i], stored.at[i]))
+        for j in range(PIECES):
+            at = pl.ds(j * (TOK // PIECES), TOK // PIECES)
+            loads.append(
+                pltpu.make_async_copy(sources[i].at[at], held[i].at[at], loaded.at[i, j])
+            )
+            stores.append(
+                pltpu.make_async_copy(held[i].at[at], targets[i].at[at], stored.at[i, j])
+            )
     for copy in loads:
         copy.start()
     query_gain[...] = gains[0:1]
@@ -437,7 +465,7 @@
             pltpu.VMEM((KV, 8, WIDTH), jnp.float32),
             pltpu.VMEM((BLOCKS * TOK, WIDTH), jnp.bfloat16),
             pltpu.VMEM((BLOCKS * TOK, WIDTH), jnp.bfloat16),
-            pltpu.VMEM((KV, BLOCKS, 2 * TOK, HEAD), jnp.float32),
+            pltpu.VMEM((KV, SPAN, 2 * TOK, HEAD), jnp.float32),
             pltpu.VMEM((KV, SPAN, 2 * TOK, HEAD), jnp.bfloat16),
             pltpu.VMEM((KV, SPAN, 2 * TOK, HEAD), jnp.bfloat16),
             pltpu.VMEM(wide, jnp.bfloat16),
@@ -488,8 +516,8 @@
             pltpu.VMEM(wide, jnp.bfloat16),
             pltpu.VMEM(narrow, jnp.bfloat16),
             pltpu.VMEM(narrow, jnp.bfloat16),
-            dma((4,)),
-            dma((4,)),
+            dma((4, PIECES)),
+            dma((4, PIECES)),
         ],
         name="deliver",
     )(*outs)

time: 115 us -> 111 us (0.965)
  Pallas kernels: 114 us -> 109 us
    pallas_call x1, Pallas kernels: 110 us -> 105 us  [local(): pl.pallas_call(kernel, out_shape=outs_like, in_specs=[hbm, hbm, hbm, vmem...]
where the time goes in v3:
time: 111 us; the launch traced here: 109 us
  Pallas kernels  109 us (98%)
    pallas_call x1, Pallas kernels, local(): pl.pallas_call(kernel, out_shape=outs_like, in_specs=[hbm, hbm, hbm, vmem...  105 us
    pallas_call x1, Pallas kernels, local(): pl.pallas_call(deliver, out_shape=outs_like[:4] + (jax.ShapeDtypeStruct((...  3.59 us

profile of v3, /device:TPU:24, one launch (start us, length us, event | category | flops | bytes accessed | tf_op | source)
XLA Modules:
  0.0 109.3 jit_solution(13131387776196658865)
XLA Ops:
  0.6 105.0 %attention.1 = (bf16[128,2560]{1,0:T(8,128)(2,1)}, bf16[128,2560]{1,0:T(8,128)(2,1)}, bf16[128,512]{1,0:T(8,128)(2,1)}, bf16[128,512]{1,0:T(8,128)(2,1)}, f32[2,128]{1,0:T(2,128)}) custom-call(bf16[128,2560]{1,0:T(8,128)(2,1)} %bitcast.12, bf16[128,512]{1,0:T(8,128)(2,1)} %bitcast.16, bf16[128,512]{1,0:T(8,128)(2,1)} %bitcast.17, f32[1,128]{1,0:T(1,128)} %bitcast.20, ...), custom_call_target="tpu_custom_call" | custom-call | flops 4026531840 | bytes 3145728 | tf_op jit(solution)/shard_map/attention/pallas_call | solution.py:450
  105.7 3.6 %deliver.1 = (bf16[128,2560]{1,0:T(8,128)(2,1)}, bf16[128,2560]{1,0:T(8,128)(2,1)}, bf16[128,512]{1,0:T(8,128)(2,1)}, bf16[128,512]{1,0:T(8,128)(2,1)}, f32[1,128]{1,0:T(1,128)}, /*index=5*/f32[1,128]{1,0:T(1,128)}) custom-call(bf16[128,2560]{1,0:T(8,128)(2,1)} %get-tuple-element.17.refs_0_, bf16[128,2560]{1,0:T(8,128)(2,1)} %get-tuple-element.18.refs_1_, ...), custom_call_target="tpu_custom_call" | custom-call | tf_op jit(solution)/shard_map/deliver/pallas_call | solution.py:509

commit v4 on v3

--- a/solution.py
+++ b/solution.py
@@ -14,6 +14,7 @@
 KV = 4
 GROUP = 5
 OFFSETS = (0, 0, 7, 7)
+LATE = (1, 1, 0, 0)
 ROW = 16
 WIDTH = GROUP * TOK
 ROUNDS = OFFSETS[-1] + 2 * SPAN + 1
@@ -21,7 +22,6 @@
 SWAPS = (0, 1, 2, 3, 5, 6)
 EPSILON = 1e-06
 LIMIT = 60
-PIECES = 4
 SCALE = HEAD**-0.5
 MESH = pl.DeviceIdType.MESH
 
@@ -50,11 +50,13 @@
 
 def kernel(
     query_hbm, key_hbm, value_hbm, query_gain_ref, key_gain_ref, segment_ref, grad_hbm,
-    attended_hbm, grad_query_hbm, grad_key_hbm, grad_value_hbm, gains_ref,
-    window, ids, bias, query_norm, grad_rows, grad_cols, key_norm, key_unit, scores, row_max,
+    attended_hbm, grad_query_hbm, grad_key_hbm, grad_value_hbm, query_gain_hbm,
+    key_gain_hbm,
+    window, ids, bias, query_norm, grad_rows, grad_cols, key_norm, key_unit, scores, tops, totals, factors,
+    corrections, outputs,
     weights, grad_scores, partial, outgoing, incoming,
-    query_ref, grad_ref, attended_ref, grad_query_ref, grad_key_ref, grad_value_ref, sums, exchange,
-    up_send, up_recv, id_send, id_recv, down_send, down_recv, swap_send, swap_recv, load, wide_store, narrow_store,
+    query_ref, grad_ref, attended_ref, grad_query_ref, grad_key_ref, grad_value_ref, sums, exchange, gains,
+    up_send, up_recv, id_send, id_recv, down_send, down_recv, swap_send, swap_recv, load, wide_store, narrow_store, gain_store,
 ):
     count = lax.axis_size("seq")
     me = lax.axis_index("seq")
@@ -192,63 +194,69 @@
         for member in range(GROUP):
             at = slice(member * TOK, (member + 1) * TOK)
             part = raw[:, at] + block_bias
+            top = jnp.max(part, axis=0, keepdims=True)
+            part = jnp.exp2(part - top)
             scores[head, step, :, at] = part
-            top = jnp.max(part.reshape(TOK // 8, 8, TOK), axis=0)
-            row_max[head, :, at] = jnp.maximum(row_max[head, :, at], top)
-
-    def head_work(head):
-        top = jnp.max(row_max[head], axis=0, keepdims=True)
-
-        def exponent(step, total):
-            part = jnp.exp2(scores[head, step] - top)
-            scores[head, step] = part
-            return total + jnp.sum(part.reshape(TOK // 8, 8, WIDTH), axis=0)
-
-        total = lax.fori_loop(0, BLOCKS, exponent, jnp.zeros((8, WIDTH), jnp.float32))
-        inverse = 1.0 / jnp.sum(total, axis=0, keepdims=True)
-        near, rows = SPAN * TOK, BLOCKS * TOK
-
-        weights[near:] = (scores[head, SPAN] * inverse).astype(jnp.bfloat16)
-        grad_value = dot(weights[near:], grad_rows[head], NN)
+            tops[head, step, :, at] = top
+            totals[head, step, :, at] = jnp.sum(part, axis=0, keepdims=True)
+
+    near, rows = SPAN * TOK, BLOCKS * TOK
+
+    def weigh_block(head):
+        top = jnp.max(tops[head], axis=0, keepdims=True)
+        factor = jnp.exp2(tops[head] - top)
+        factor = factor / jnp.sum(factor * totals[head], axis=0, keepdims=True)
+        factors[head] = factor
+        at = lax.rem(head, 2)
+        weights[at, near:] = (scores[head, SPAN] * factor[SPAN]).astype(jnp.bfloat16)
+        grad_value = dot(weights[at, near:], grad_rows[head], NN)
         outgoing[head, 0, TOK:] = grad_value.astype(jnp.bfloat16)
         down(head, 0, 1).start()
 
-        weights[:near] = (scores[head, :SPAN].reshape(near, WIDTH) * inverse).astype(jnp.bfloat16)
-        output = dot(window[head, :, TOK:].reshape(rows, HEAD), weights[...], TN)
-        output = output.astype(jnp.bfloat16).astype(jnp.float32)
-        correction = jnp.sum(output * grad_cols[head].astype(jnp.float32), axis=0, keepdims=True)
-        scaled = inverse * SCALE
-
+    def attend(head):
+        at = lax.rem(head, 2)
+        weights[at, :near] = (
+            (scores[head, :SPAN] * factors[head, :SPAN]).reshape(near, WIDTH).astype(jnp.bfloat16)
+        )
+        output = dot(window[head, :, TOK:].reshape(rows, HEAD), weights[at], TN)
+        output = output.astype(jnp.bfloat16)
+        outputs[at] = output
+        correction = jnp.sum(
+            output.astype(jnp.float32) * grad_cols[head].astype(jnp.float32), axis=0, keepdims=True
+        )
+        corrections[head] = correction
         grad_prob = dot(window[head, SPAN, TOK:], grad_rows[head], NT)
-        grad_scores[near:] = (
-            scores[head, SPAN] * scaled * (grad_prob - correction)
+        grad_scores[at, near:] = (
+            scores[head, SPAN] * (factors[head, SPAN] * SCALE) * (grad_prob - correction)
         ).astype(jnp.bfloat16)
-        grad_key = dot(grad_scores[near:], query_norm[head], NN)
+        grad_key = dot(grad_scores[at, near:], query_norm[head], NN)
         outgoing[head, 0, :TOK] = grad_key.astype(jnp.bfloat16)
         down(head, 0, 0).start()
         sums[8:] += jnp.sum((grad_key * key_unit[head, SPAN]).reshape(-1, 8, HEAD), axis=0)
 
-        grad_value = dot(weights[:near], grad_rows[head], NN)
+    def head_rest(head):
+        at = lax.rem(head, 2)
+        grad_value = dot(weights[at, :near], grad_rows[head], NN)
         partial[head, :, TOK:] = grad_value.reshape(SPAN, TOK, HEAD)
         value_rows = window[head, :SPAN, TOK:].reshape(near, HEAD)
         grad_prob = dot(value_rows, grad_rows[head], NT)
-        grad_scores[:near] = (
-            scores[head, :SPAN].reshape(near, WIDTH) * scaled * (grad_prob - correction)
-        ).astype(jnp.bfloat16)
-        grad_key = dot(grad_scores[:near], query_norm[head], NN)
+        scaled = (scores[head, :SPAN] * (factors[head, :SPAN] * SCALE)).reshape(near, WIDTH)
+        grad_scores[at, :near] = (scaled * (grad_prob - corrections[head])).astype(jnp.bfloat16)
+        grad_key = dot(grad_scores[at, :near], query_norm[head], NN)
         partial[head, :, :TOK] = grad_key.reshape(SPAN, TOK, HEAD)
         units = key_unit[head, :SPAN].reshape(near, HEAD)
         sums[8:] += jnp.sum((grad_key * units).reshape(-1, 8, HEAD), axis=0)
+        output = outputs[at].astype(jnp.float32)
 
         for member in range(GROUP):
-            at = slice(member * TOK, (member + 1) * TOK)
-            attended_ref[:, lanes(head * GROUP + member)] = output[:, at].T.astype(jnp.bfloat16)
-        grad_query = dot(key_norm[head].reshape(rows, HEAD), grad_scores[...], TN)
+            cols = slice(member * TOK, (member + 1) * TOK)
+            attended_ref[:, lanes(head * GROUP + member)] = output[:, cols].T.astype(jnp.bfloat16)
+        grad_query = dot(key_norm[head].reshape(rows, HEAD), grad_scores[at], TN)
         for member in range(GROUP):
-            at = slice(member * TOK, (member + 1) * TOK)
+            cols = slice(member * TOK, (member + 1) * TOK)
             where = lanes(head * GROUP + member)
             unit, query_inverse = normalize(query_ref[:, where].astype(jnp.float32))
-            grad = grad_query[:, at].T
+            grad = grad_query[:, cols].T
             sums[:8] += jnp.sum((grad * unit).reshape(TOK // 8, 8, HEAD), axis=0)
             grad_query_ref[:, where] = norm_backward(
                 grad, unit, query_inverse, query_gain_ref[...]
@@ -270,10 +278,10 @@
             source.at[:, at], target.at[:, at], wide_store.at[head, part]
         )
 
-    def receive_up(head, step):
+    def receive_up(head, step, part):
         @pl.when((step >= 0) & (step <= SPAN))
         def _():
-            if head == 0:
+            if head == 0 and part == 0:
 
                 @pl.when(step > 0)
                 def _():
@@ -283,41 +291,39 @@
                 def _():
                     up_ids(step).start()
 
-            for part in range(2):
-
-                @pl.when(step > 0)
-                def _():
-                    up(head, step - 1, part).wait_recv()
-
-                @pl.when(step < SPAN)
-                def _():
-                    up(head, step, part).start()
-
-    def receive_down(head, back):
-        @pl.when((back >= 1) & (back < SPAN))
+            @pl.when(step > 0)
+            def _():
+                up(head, step - 1, part).wait_recv()
+
+            @pl.when(step < SPAN)
+            def _():
+                up(head, step, part).start()
+
+    def receive_down(head, back, part):
+        rows = slice(part * TOK, (part + 1) * TOK)
+
+        @pl.when((back >= 1) & (back <= SPAN))
         def _():
-            for part in (1, 0):
-                rows = slice(part * TOK, (part + 1) * TOK)
-                down(head, back - 1, part).wait_recv()
-                total = incoming[head, back - 1, rows].astype(jnp.float32)
-                total = total + partial[head, SPAN - back, rows]
+            down(head, back - 1, part).wait_recv()
+            total = incoming[head, back - 1, rows].astype(jnp.float32)
+            total = total + partial[head, SPAN - back, rows]
+
+            @pl.when(back < SPAN)
+            def _():
                 outgoing[head, back, rows] = total.astype(jnp.bfloat16)
                 down(head, back, part).start()
 
-        @pl.when(back == SPAN)
-        def _():
-            at = slice(head * HEAD, (head + 1) * HEAD)
-            down(head, SPAN - 1, 1).wait_recv()
-            total = incoming[head, SPAN - 1, TOK:].astype(jnp.float32) + partial[head, 0, TOK:]
-            grad_value_ref[:, at] = total.astype(jnp.bfloat16)
-            narrow(head, 1).start()
-            down(head, SPAN - 1, 0).wait_recv()
-            total = incoming[head, SPAN - 1, :TOK].astype(jnp.float32) + partial[head, 0, :TOK]
-            unit, inverse = normalize(window[head, 0, :TOK].astype(jnp.float32))
-            grad_key_ref[:, at] = norm_backward(
-                total, unit, inverse, key_gain_ref[...]
-            ).astype(jnp.bfloat16)
-            narrow(head, 0).start()
+            @pl.when(back == SPAN)
+            def _():
+                at = slice(head * HEAD, (head + 1) * HEAD)
+                if part == 1:
+                    grad_value_ref[:, at] = total.astype(jnp.bfloat16)
+                else:
+                    unit, inverse = normalize(window[head, 0, :TOK].astype(jnp.float32))
+                    grad_key_ref[:, at] = norm_backward(
+                        total, unit, inverse, key_gain_ref[...]
+                    ).astype(jnp.bfloat16)
+                narrow(head, part).start()
 
     def work(head, step):
         @pl.when((step >= 1) & (step <= SPAN))
@@ -328,13 +334,11 @@
 
             score_block(head, step)
 
-        @pl.when(step == SPAN)
-        def _():
-            head_work(head)
-            wide(head, 0).start()
-            wide(head, 1).start()
-
-    row_max[...] = jnp.full(row_max.shape, -jnp.inf, jnp.float32)
+    def whole(head):
+        head_rest(head)
+        wide(head, 0).start()
+        wide(head, 1).start()
+
     sums[...] = jnp.zeros(sums.shape, jnp.float32)
     for copy in loads[:-2]:
         copy.wait()
@@ -360,8 +364,12 @@
         )
 
     def one_round(index, carry):
-        for head in range(KV):
-            receive_up(head, index - OFFSETS[head])
+        for place_in_pair in range(2):
+            for part in range(2):
+                for head in (place_in_pair + 2, place_in_pair):
+                    step = index - OFFSETS[head]
+                    receive_up(head, step, part)
+                    receive_down(head, step - SPAN - LATE[head], 1 - part)
 
         def second(head, inner):
             work(head, index - offset(head))
@@ -372,8 +380,17 @@
             ready(index)
 
         lax.fori_loop(0, KV, second, 0)
-        for head in range(KV):
-            receive_down(head, index - OFFSETS[head] - SPAN)
+        for stage, late in ((weigh_block, 0), (attend, 0), (whole, LATE[0])):
+
+            def third(head, inner, stage=stage, late=late):
+                @pl.when(index == offset(head) + SPAN + jnp.where(head < 2, late, 0))
+                def _():
+                    stage(head)
+
+                return inner
+
+            lax.fori_loop(0, KV, third, 0)
+
 
         for phase in range(6):
 
@@ -407,27 +424,21 @@
         for part in range(2):
             wide(head, part).wait()
             narrow(head, part).wait()
-    gains_ref[...] = jnp.sum(sums[...].reshape(2, 8, HEAD), axis=1)
+    for part, target in enumerate((query_gain_hbm, key_gain_hbm)):
+        gains[part] = jnp.sum(sums[part * 8 : part * 8 + 8], axis=0, keepdims=True)
+        pltpu.make_async_copy(gains.at[part], target, gain_store.at[part]).start()
+    for part, target in enumerate((query_gain_hbm, key_gain_hbm)):
+        pltpu.make_async_copy(gains.at[part], target, gain_store.at[part]).wait()
 
 
 def deliver(*refs):
-    sources, gains, targets = refs[:4], refs[4], refs[5:9]
-    query_gain, key_gain = refs[9:11]
-    held, loaded, stored = refs[11:15], refs[15], refs[16]
     loads, stores = [], []
-    for i in range(4):
-        for j in range(PIECES):
-            at = pl.ds(j * (TOK // PIECES), TOK // PIECES)
-            loads.append(
-                pltpu.make_async_copy(sources[i].at[at], held[i].at[at], loaded.at[i, j])
-            )
-            stores.append(
-                pltpu.make_async_copy(held[i].at[at], targets[i].at[at], stored.at[i, j])
-            )
+    for i in range(6):
+        source, target, held = refs[i], refs[6 + i], refs[12 + i]
+        loads.append(pltpu.make_async_copy(source, held, refs[18].at[i]))
+        stores.append(pltpu.make_async_copy(held, target, refs[19].at[i]))
     for copy in loads:
         copy.start()
-    query_gain[...] = gains[0:1]
-    key_gain[...] = gains[1:2]
     for load, store in zip(loads, stores):
         load.wait()
         store.start()
@@ -445,13 +456,12 @@
         jax.ShapeDtypeStruct(wide, jnp.bfloat16),
         jax.ShapeDtypeStruct(narrow, jnp.bfloat16),
         jax.ShapeDtypeStruct(narrow, jnp.bfloat16),
-        jax.ShapeDtypeStruct((2, HEAD), jnp.float32),
-    )
+    ) + (jax.ShapeDtypeStruct((1, HEAD), jnp.float32),) * 2
     outs = pl.pallas_call(
         kernel,
         out_shape=outs_like,
         in_specs=[hbm, hbm, hbm, vmem, vmem, vmem, hbm],
-        out_specs=(hbm,) * 4 + (vmem,),
+        out_specs=(hbm,) * 6,
         scratch_shapes=[
             pltpu.VMEM((KV, BLOCKS, 2 * TOK, HEAD), jnp.bfloat16),
             pltpu.VMEM((BLOCKS, 16, TOK), jnp.bfloat16),
@@ -462,9 +472,13 @@
             pltpu.VMEM((KV, BLOCKS, TOK, HEAD), jnp.bfloat16),
             pltpu.VMEM((KV, BLOCKS, TOK, HEAD), jnp.float32),
             pltpu.VMEM((KV, BLOCKS, TOK, WIDTH), jnp.float32),
-            pltpu.VMEM((KV, 8, WIDTH), jnp.float32),
-            pltpu.VMEM((BLOCKS * TOK, WIDTH), jnp.bfloat16),
-            pltpu.VMEM((BLOCKS * TOK, WIDTH), jnp.bfloat16),
+            pltpu.VMEM((KV, BLOCKS, 1, WIDTH), jnp.float32),
+            pltpu.VMEM((KV, BLOCKS, 1, WIDTH), jnp.float32),
+            pltpu.VMEM((KV, BLOCKS, 1, WIDTH), jnp.float32),
+            pltpu.VMEM((KV, 1, WIDTH), jnp.float32),
+            pltpu.VMEM((2, HEAD, WIDTH), jnp.bfloat16),
+            pltpu.VMEM((2, BLOCKS * TOK, WIDTH), jnp.bfloat16),
+            pltpu.VMEM((2, BLOCKS * TOK, WIDTH), jnp.bfloat16),
             pltpu.VMEM((KV, SPAN, 2 * TOK, HEAD), jnp.float32),
             pltpu.VMEM((KV, SPAN, 2 * TOK, HEAD), jnp.bfloat16),
             pltpu.VMEM((KV, SPAN, 2 * TOK, HEAD), jnp.bfloat16),
@@ -476,6 +490,7 @@
             pltpu.VMEM(narrow, jnp.bfloat16),
             pltpu.VMEM((16, HEAD), jnp.float32),
             pltpu.VMEM((4, 8, 16, HEAD), jnp.float32),
+            pltpu.VMEM((2, 1, HEAD), jnp.float32),
             dma((KV, SPAN, 2)),
             dma((KV, SPAN, 2)),
             dma((SPAN,)),
@@ -487,6 +502,7 @@
             dma((2 * KV + 2,)),
             dma((KV, 2)),
             dma((KV, 2)),
+            dma((2,)),
         ],
         compiler_params=pltpu.CompilerParams(
             collective_id=0, has_side_effects=True, vmem_limit_bytes=LIMIT << 20
@@ -508,17 +524,11 @@
     )
     attended, grad_query, grad_key, grad_values, grad_query_gain, grad_key_gain = pl.pallas_call(
         deliver,
-        out_shape=outs_like[:4] + (jax.ShapeDtypeStruct((1, HEAD), jnp.float32),) * 2,
-        in_specs=[hbm] * 4 + [vmem],
-        out_specs=(hbm,) * 4 + (vmem,) * 2,
-        scratch_shapes=[
-            pltpu.VMEM(wide, jnp.bfloat16),
-            pltpu.VMEM(wide, jnp.bfloat16),
-            pltpu.VMEM(narrow, jnp.bfloat16),
-            pltpu.VMEM(narrow, jnp.bfloat16),
-            dma((4, PIECES)),
-            dma((4, PIECES)),
-        ],
+        out_shape=outs_like,
+        in_specs=[hbm] * 6,
+        out_specs=(hbm,) * 6,
+        scratch_shapes=[pltpu.VMEM(like.shape, like.dtype) for like in outs_like]
+        + [dma((6,)), dma((6,))],
         name="deliver",
     )(*outs)
     return (

time: 111 us -> 107 us (0.964)
  Pallas kernels: 109 us -> 105 us
    pallas_call x1, Pallas kernels: 105 us -> 102 us  [local(): pl.pallas_call(kernel, out_shape=outs_like, in_specs=[hbm, hbm, hbm, vmem...]
    pallas_call x1, Pallas kernels: 3.59 us -> 2.33 us  [local(): pl.pallas_call(deliver, out_shape=outs_like, in_specs=[hbm] * 6, out_spec...]
where the time goes in v4:
time: 107 us; the launch traced here: 105 us
  Pallas kernels  105 us (98%)
    pallas_call x1, Pallas kernels, local(): pl.pallas_call(kernel, out_shape=outs_like, in_specs=[hbm, hbm, hbm, vmem...  102 us
    pallas_call x1, Pallas kernels, local(): pl.pallas_call(deliver, out_shape=outs_like, in_specs=[hbm] * 6, out_spec...  2.33 us

profile of v4, /device:TPU:24, one launch (start us, length us, event | category | flops | bytes accessed | tf_op | source)
XLA Modules:
  0.0 105.4 jit_solution(1025829523310767614)
XLA Ops:
  0.6 102.5 %attention.1 = (bf16[128,2560]{1,0:T(8,128)(2,1)}, bf16[128,2560]{1,0:T(8,128)(2,1)}, bf16[128,512]{1,0:T(8,128)(2,1)}, bf16[128,512]{1,0:T(8,128)(2,1)}, f32[1,128]{1,0:T(1,128)}, /*index=5*/f32[1,128]{1,0:T(1,128)}) custom-call(bf16[128,2560]{1,0:T(8,128)(2,1)} %bitcast.12, bf16[128,512]{1,0:T(8,128)(2,1)} %bitcast.16, bf16[128,512]{1,0:T(8,128)(2,1)} %bitcast.17, ...), custom_call_target="tpu_custom_call" | custom-call | flops 4026531840 | bytes 3145728 | tf_op jit(solution)/shard_map/attention/pallas_call | solution.py:460
  103.1 2.3 %deliver.1 = (bf16[128,2560]{1,0:T(8,128)(2,1)}, bf16[128,2560]{1,0:T(8,128)(2,1)}, bf16[128,512]{1,0:T(8,128)(2,1)}, bf16[128,512]{1,0:T(8,128)(2,1)}, f32[1,128]{1,0:T(1,128)}, /*index=5*/f32[1,128]{1,0:T(1,128)}) custom-call(bf16[128,2560]{1,0:T(8,128)(2,1)} %get-tuple-element.18.refs_0_, bf16[128,2560]{1,0:T(8,128)(2,1)} %get-tuple-element.19.refs_1_, ...), custom_call_target="tpu_custom_call" | custom-call | tf_op jit(solution)/shard_map/deliver/pallas_call | solution.py:525

commit v5 on v4

--- a/solution.py
+++ b/solution.py
@@ -73,17 +73,6 @@
             return at, me
         return dp, me + (at - mine[phase]) * (0, ROW, 1, 4)[phase]
 
-    loads = []
-    for head in range(KV):
-        at = slice(head * HEAD, (head + 1) * HEAD)
-        loads.append((key_hbm.at[:, at], window.at[head, 0, pl.ds(0, TOK)]))
-        loads.append((value_hbm.at[:, at], window.at[head, 0, pl.ds(TOK, TOK)]))
-    loads.append((query_hbm, query_ref))
-    loads.append((grad_hbm, grad_ref))
-    loads = [pltpu.make_async_copy(a, b, load.at[i]) for i, (a, b) in enumerate(loads)]
-    for copy in loads:
-        copy.start()
-
     barrier = pltpu.get_barrier_semaphore()
     greeted = 2
     for neighbour in (after, before):
@@ -95,6 +84,17 @@
             target = peer(phase, lax.rem(mine[phase] + j, sizes[phase]))
             pl.semaphore_signal(barrier, inc=1, device_id=target, device_id_type=MESH)
             greeted += 1
+
+    loads = []
+    for head in range(KV):
+        at = slice(head * HEAD, (head + 1) * HEAD)
+        loads.append((key_hbm.at[:, at], window.at[head, 0, pl.ds(0, TOK)]))
+        loads.append((value_hbm.at[:, at], window.at[head, 0, pl.ds(TOK, TOK)]))
+    loads.append((query_hbm, query_ref))
+    loads.append((grad_hbm, grad_ref))
+    loads = [pltpu.make_async_copy(a, b, load.at[i]) for i, (a, b) in enumerate(loads)]
+    for copy in loads:
+        copy.start()
 
     def swap(phase, j, slot):
         return pltpu.make_async_remote_copy(
@@ -342,7 +342,6 @@
     sums[...] = jnp.zeros(sums.shape, jnp.float32)
     for copy in loads[:-2]:
         copy.wait()
-    pl.semaphore_wait(barrier, greeted)
 
     def ready(head):
         def one(member, carry):
@@ -357,6 +356,9 @@
 
         lax.fori_loop(0, GROUP, one, 0)
         score_block(head, 0)
+
+    ready(0)
+    pl.semaphore_wait(barrier, greeted)
 
     def offset(head):
         return sum(
@@ -375,9 +377,9 @@
             work(head, index - offset(head))
             return inner
 
-        @pl.when(index < KV)
+        @pl.when(index < KV - 1)
         def _():
-            ready(index)
+            ready(index + 1)
 
         lax.fori_loop(0, KV, second, 0)
         for stage, late in ((weigh_block, 0), (attend, 0), (whole, LATE[0])):

time: 107 us -> 106 us (level)
  no operation moved by 1% of the time
where the time goes in v5:
time: 106 us; the launch traced here: 105 us
  Pallas kernels  104 us (98%)
    pallas_call x1, Pallas kernels, local(): pl.pallas_call(kernel, out_shape=outs_like, in_specs=[hbm, hbm, hbm, vmem...  102 us
    pallas_call x1, Pallas kernels, local(): pl.pallas_call(deliver, out_shape=outs_like, in_specs=[hbm] * 6, out_spec...  2.33 us

profile of v5, /device:TPU:24, one launch (start us, length us, event | category | flops | bytes accessed | tf_op | source)
XLA Modules:
  0.0 104.8 jit_solution(12647974723149822932)
XLA Ops:
  0.6 101.8 %attention.1 = (bf16[128,2560]{1,0:T(8,128)(2,1)}, bf16[128,2560]{1,0:T(8,128)(2,1)}, bf16[128,512]{1,0:T(8,128)(2,1)}, bf16[128,512]{1,0:T(8,128)(2,1)}, f32[1,128]{1,0:T(1,128)}, /*index=5*/f32[1,128]{1,0:T(1,128)}) custom-call(bf16[128,2560]{1,0:T(8,128)(2,1)} %bitcast.12, bf16[128,512]{1,0:T(8,128)(2,1)} %bitcast.16, bf16[128,512]{1,0:T(8,128)(2,1)} %bitcast.17, ...), custom_call_target="tpu_custom_call" | custom-call | flops 4026531840 | bytes 3145728 | tf_op jit(solution)/shard_map/attention/pallas_call | solution.py:462
  102.5 2.3 %deliver.1 = (bf16[128,2560]{1,0:T(8,128)(2,1)}, bf16[128,2560]{1,0:T(8,128)(2,1)}, bf16[128,512]{1,0:T(8,128)(2,1)}, bf16[128,512]{1,0:T(8,128)(2,1)}, f32[1,128]{1,0:T(1,128)}, /*index=5*/f32[1,128]{1,0:T(1,128)}) custom-call(bf16[128,2560]{1,0:T(8,128)(2,1)} %get-tuple-element.18.refs_0_, bf16[128,2560]{1,0:T(8,128)(2,1)} %get-tuple-element.19.refs_1_, ...), custom_call_target="tpu_custom_call" | custom-call | tf_op jit(solution)/shard_map/deliver/pallas_call | solution.py:527
